TPU v7x, 512 devices: a whole 4x4x16 slice. The times are simulated.
512 devices in a mesh: seq: 64 (over x, y, z_hi, core), chan: 8 (over z_lo).
Axes of the slice: x: 4, y: 4, z: 16 (z_hi: 2, z_lo: 8; z = z_hi * 8 + z_lo), core: 2. Of those that a mesh axis runs over, the one named last changes fastest.
Arguments:
- tokens: bfloat16 [16384, 4096], P('seq', 'chan'), may hold values from -6 to 6
- w_in: bfloat16 [4096, 3, 4096], P('seq', None, 'chan'), may hold values from -0.09375 to 0.09375
- short_taps: float32 [3, 3, 4096], P(None, None, 'chan'), may hold values from -3 to 3
- residues: float32 [16, 4096], P(None, 'chan'), may hold values from -0.046875 to 0.046875
- poles: float32 [16, 4096], P(None, 'chan'), may hold values from 0.3 to 512
- skip_gain: float32 [4096], P('chan'), may hold values from 0.5 to 1.5
Outputs:
- mixed: bfloat16 [16384, 4096], P('seq', 'chan')
All inputs are finite; a program needn't handle non-finite values.
Results may differ from a plain program's by a relative error of at most 0.008.
Values may be sent and summed in bfloat16 or wider, within the bound.
A program may use at most 64 MiB of HBM per device.

v0:
```python
import jax
import jax.numpy as jnp
from jax import lax
from jax.sharding import PartitionSpec as P

HIGHEST = lax.Precision.HIGHEST
THREEPASS = lax.Precision.HIGH


def from_behind(value, axis, by):
    length = lax.axis_size(axis)
    pairs = [(i, i + by) for i in range(length) if 0 <= i + by < length]
    return lax.ppermute(value, axis, pairs)


def modal_filter(count, length, residues, poles):
    scaled = jnp.arange(count, dtype=jnp.float32) / length
    total = jnp.zeros((count, residues.shape[1]), jnp.float32)
    for mode in range(residues.shape[0]):
        total = total + residues[mode][None, :] * jnp.exp(-poles[mode][None, :] * scaled[:, None])
    return total


def short_filter(projected, previous, taps):
    extended = jnp.concatenate([previous, projected], axis=0).astype(jnp.float32)
    return taps[0] * extended[2:] + taps[1] * extended[1:-1] + taps[2] * extended[:-2]


def local_conv(gated, filter_taps, tok_rows):
    span = 2 * tok_rows
    bins = tok_rows + 1
    bin_index = jnp.arange(bins, dtype=jnp.int32)
    phase = bin_index[:, None] * jnp.arange(tok_rows, dtype=jnp.int32)[None, :] % span
    angles = phase.astype(jnp.float32) * (2.0 * jnp.pi / span)
    cos_table = jnp.cos(angles)
    sin_table = jnp.sin(angles)
    filt_real = jnp.dot(cos_table, filter_taps, precision=HIGHEST)
    filt_imag = -jnp.dot(sin_table, filter_taps, precision=HIGHEST)
    data = gated.astype(jnp.float32)
    data_real = jnp.dot(cos_table, data, precision=THREEPASS)
    data_imag = -jnp.dot(sin_table, data, precision=THREEPASS)
    prod_real = filt_real * data_real - filt_imag * data_imag
    prod_imag = filt_real * data_imag + filt_imag * data_real
    edge = (bin_index == 0) | (bin_index == tok_rows)
    bin_weight = jnp.where(edge, 1.0, 2.0).astype(jnp.float32) / span
    inv_cos = (cos_table * bin_weight[:, None]).T
    inv_sin = (sin_table * bin_weight[:, None]).T
    return jnp.dot(inv_cos, prod_real, precision=THREEPASS) - jnp.dot(
        inv_sin, prod_imag, precision=THREEPASS
    )


def earlier_states(gated, poles, tok_rows, length):
    offsets = jnp.arange(tok_rows, dtype=jnp.float32)
    data = gated.astype(jnp.float32)
    ends = []
    for mode in range(poles.shape[0]):
        weights = jnp.exp(-poles[mode][None, :] * ((tok_rows - 1 - offsets)[:, None] / length))
        ends.append(jnp.sum(weights * data, axis=0))
    states = jnp.stack(ends)
    block_decay = jnp.exp(-poles * (tok_rows / length))

    def step_once(index, carried):
        return from_behind(carried * block_decay + states, "seq", 1)

    return lax.fori_loop(0, lax.axis_size("seq") - 1, step_once, jnp.zeros_like(states))


def long_conv(gated, residues, poles, tok_rows):
    length = float(tok_rows * lax.axis_size("seq"))
    carried = earlier_states(gated, poles, tok_rows, length)
    filter_taps = modal_filter(tok_rows, length, residues, poles)
    result = local_conv(gated, filter_taps, tok_rows)
    offsets = jnp.arange(tok_rows, dtype=jnp.float32)
    for mode in range(poles.shape[0]):
        weights = jnp.exp(-poles[mode][None, :] * ((offsets + 1.0)[:, None] / length))
        result = result + (residues[mode] * carried[mode])[None, :] * weights
    return result


def local(tokens, w_in, short_taps, residues, poles, skip_gain):
    whole = lax.all_gather(tokens, "chan", axis=1, tiled=True)
    tok_rows = whole.shape[0]
    projected = jnp.einsum(
        "td,dgc->tgc",
        whole,
        lax.all_gather(w_in, "seq", axis=0, tiled=True),
        preferred_element_type=jnp.float32,
    ).astype(jnp.bfloat16)
    previous = from_behind(projected[-2:], "seq", 1)
    smoothed = short_filter(projected, previous, short_taps)
    query = smoothed[:, 0]
    gated = (smoothed[:, 1] * smoothed[:, 2]).astype(jnp.bfloat16)
    convolved = long_conv(gated, residues, poles, tok_rows)
    return (query * (convolved + skip_gain * gated.astype(jnp.float32))).astype(jnp.bfloat16)


def solution(mesh):
    placed = (
        P("seq", "chan"),
        P("seq", None, "chan"),
        P(None, None, "chan"),
        P(None, "chan"),
        P(None, "chan"),
        P("chan"),
    )
    return jax.shard_map(
        local, mesh=mesh, in_specs=placed, out_specs=P("seq", "chan"), check_vma=False
    )
```

profile of v0, /device:TPU:100, one launch (start us, length us, event | category | flops | bytes accessed | tf_op | source)
XLA Modules:
  0.0 1418.7 jit_solution(8787787162916174333)
XLA Ops:
  11.7 59.9 %all-gather.3.cloned.1.call-done = bf16[256,4096]{1,0:T(8,128)(2,1)} async-done(((bf16[256,512]{1,0:T(8,128)(2,1)}), bf16[256,4096]{1,0:T(8,128)(2,1)}) %all-gather.3.cloned.1.call-update) | async-done | bytes 2097168 | tf_op jit(solution)/shard_map/all_gather | solution.py:82
  71.5 225.4 %all-gather.5.cloned.1.call-done = bf16[4096,3,512]{2,0,1:T(8,128)(2,1)} async-done(((bf16[64,3,512]{2,0,1:T(8,128)(2,1)}), bf16[4096,3,512]{2,0,1:T(8,128)(2,1)}) %all-gather.5.cloned.1.call-update) | async-done | bytes 12582928 | tf_op jit(solution)/shard_map/all_gather | solution.py:87
  324.6 1072.8 %while.10 = (s32[]{:T(128)}, f32[16,512]{1,0:T(8,128)S(1)}, f32[16,512]{1,0:T(8,128)S(1)}, f32[16,512]{1,0:T(8,128)S(1)}, s32[]{:T(128)}) while((s32[]{:T(128)}, f32[16,512]{1,0:T(8,128)S(1)}, f32[16,512]{1,0:T(8,128)S(1)}, f32[16,512]{1,0:T(8,128)S(1)}, s32[]{:T(128)}) %tuple.80), condition=%wide.region_17.0_spmd, body=%wide.region_16.0_spmd.sunk | while | flops 16386 | bytes 262245 | solution.py:66
  326.6 15.2 %collective-permute-done = f32[16,512]{1,0:T(8,128)S(1)} collective-permute-done((f32[16,512]{1,0:T(8,128)S(1)}, f32[16,512]{1,0:T(8,128)S(1)}, u32[]{:S(2)}, u32[]{:S(2)}) %collective-permute-start) | collective-permute-done | bytes 32800 | tf_op jit(solution)/shard_map/while/body/eval_jaxpr/ppermute | solution.py:13
  377.7 15.2 %collective-permute-done = f32[16,512]{1,0:T(8,128)S(1)} collective-permute-done((f32[16,512]{1,0:T(8,128)S(1)}, f32[16,512]{1,0:T(8,128)S(1)}, u32[]{:S(2)}, u32[]{:S(2)}) %collective-permute-start) | collective-permute-done | bytes 32800 | tf_op jit(solution)/shard_map/while/body/eval_jaxpr/ppermute | solution.py:13
  394.9 15.6 %collective-permute-done = f32[16,512]{1,0:T(8,128)S(1)} collective-permute-done((f32[16,512]{1,0:T(8,128)S(1)}, f32[16,512]{1,0:T(8,128)S(1)}, u32[]{:S(2)}, u32[]{:S(2)}) %collective-permute-start) | collective-permute-done | bytes 32800 | tf_op jit(solution)/shard_map/while/body/eval_jaxpr/ppermute | solution.py:13
  412.4 15.4 %collective-permute-done = f32[16,512]{1,0:T(8,128)S(1)} collective-permute-done((f32[16,512]{1,0:T(8,128)S(1)}, f32[16,512]{1,0:T(8,128)S(1)}, u32[]{:S(2)}, u32[]{:S(2)}) %collective-permute-start) | collective-permute-done | bytes 32800 | tf_op jit(solution)/shard_map/while/body/eval_jaxpr/ppermute | solution.py:13
  446.7 15.2 %collective-permute-done = f32[16,512]{1,0:T(8,128)S(1)} collective-permute-done((f32[16,512]{1,0:T(8,128)S(1)}, f32[16,512]{1,0:T(8,128)S(1)}, u32[]{:S(2)}, u32[]{:S(2)}) %collective-permute-start) | collective-permute-done | bytes 32800 | tf_op jit(solution)/shard_map/while/body/eval_jaxpr/ppermute | solution.py:13
  463.8 15.2 %collective-permute-done = f32[16,512]{1,0:T(8,128)S(1)} collective-permute-done((f32[16,512]{1,0:T(8,128)S(1)}, f32[16,512]{1,0:T(8,128)S(1)}, u32[]{:S(2)}, u32[]{:S(2)}) %collective-permute-start) | collective-permute-done | bytes 32800 | tf_op jit(solution)/shard_map/while/body/eval_jaxpr/ppermute | solution.py:13
  498.0 15.1 %collective-permute-done = f32[16,512]{1,0:T(8,128)S(1)} collective-permute-done((f32[16,512]{1,0:T(8,128)S(1)}, f32[16,512]{1,0:T(8,128)S(1)}, u32[]{:S(2)}, u32[]{:S(2)}) %collective-permute-start) | collective-permute-done | bytes 32800 | tf_op jit(solution)/shard_map/while/body/eval_jaxpr/ppermute | solution.py:13
  532.0 15.1 %collective-permute-done = f32[16,512]{1,0:T(8,128)S(1)} collective-permute-done((f32[16,512]{1,0:T(8,128)S(1)}, f32[16,512]{1,0:T(8,128)S(1)}, u32[]{:S(2)}, u32[]{:S(2)}) %collective-permute-start) | collective-permute-done | bytes 32800 | tf_op jit(solution)/shard_map/while/body/eval_jaxpr/ppermute | solution.py:13
  566.0 15.1 %collective-permute-done = f32[16,512]{1,0:T(8,128)S(1)} collective-permute-done((f32[16,512]{1,0:T(8,128)S(1)}, f32[16,512]{1,0:T(8,128)S(1)}, u32[]{:S(2)}, u32[]{:S(2)}) %collective-permute-start) | collective-permute-done | bytes 32800 | tf_op jit(solution)/shard_map/while/body/eval_jaxpr/ppermute | solution.py:13
  600.0 15.1 %collective-permute-done = f32[16,512]{1,0:T(8,128)S(1)} collective-permute-done((f32[16,512]{1,0:T(8,128)S(1)}, f32[16,512]{1,0:T(8,128)S(1)}, u32[]{:S(2)}, u32[]{:S(2)}) %collective-permute-start) | collective-permute-done | bytes 32800 | tf_op jit(solution)/shard_map/while/body/eval_jaxpr/ppermute | solution.py:13
  634.0 15.1 %collective-permute-done = f32[16,512]{1,0:T(8,128)S(1)} collective-permute-done((f32[16,512]{1,0:T(8,128)S(1)}, f32[16,512]{1,0:T(8,128)S(1)}, u32[]{:S(2)}, u32[]{:S(2)}) %collective-permute-start) | collective-permute-done | bytes 32800 | tf_op jit(solution)/shard_map/while/body/eval_jaxpr/ppermute | solution.py:13
  668.1 15.1 %collective-permute-done = f32[16,512]{1,0:T(8,128)S(1)} collective-permute-done((f32[16,512]{1,0:T(8,128)S(1)}, f32[16,512]{1,0:T(8,128)S(1)}, u32[]{:S(2)}, u32[]{:S(2)}) %collective-permute-start) | collective-permute-done | bytes 32800 | tf_op jit(solution)/shard_map/while/body/eval_jaxpr/ppermute | solution.py:13
  702.1 15.1 %collective-permute-done = f32[16,512]{1,0:T(8,128)S(1)} collective-permute-done((f32[16,512]{1,0:T(8,128)S(1)}, f32[16,512]{1,0:T(8,128)S(1)}, u32[]{:S(2)}, u32[]{:S(2)}) %collective-permute-start) | collective-permute-done | bytes 32800 | tf_op jit(solution)/shard_map/while/body/eval_jaxpr/ppermute | solution.py:13
  736.1 15.1 %collective-permute-done = f32[16,512]{1,0:T(8,128)S(1)} collective-permute-done((f32[16,512]{1,0:T(8,128)S(1)}, f32[16,512]{1,0:T(8,128)S(1)}, u32[]{:S(2)}, u32[]{:S(2)}) %collective-permute-start) | collective-permute-done | bytes 32800 | tf_op jit(solution)/shard_map/while/body/eval_jaxpr/ppermute | solution.py:13
  770.1 15.1 %collective-permute-done = f32[16,512]{1,0:T(8,128)S(1)} collective-permute-done((f32[16,512]{1,0:T(8,128)S(1)}, f32[16,512]{1,0:T(8,128)S(1)}, u32[]{:S(2)}, u32[]{:S(2)}) %collective-permute-start) | collective-permute-done | bytes 32800 | tf_op jit(solution)/shard_map/while/body/eval_jaxpr/ppermute | solution.py:13
  804.1 15.1 %collective-permute-done = f32[16,512]{1,0:T(8,128)S(1)} collective-permute-done((f32[16,512]{1,0:T(8,128)S(1)}, f32[16,512]{1,0:T(8,128)S(1)}, u32[]{:S(2)}, u32[]{:S(2)}) %collective-permute-start) | collective-permute-done | bytes 32800 | tf_op jit(solution)/shard_map/while/body/eval_jaxpr/ppermute | solution.py:13
  838.1 15.1 %collective-permute-done = f32[16,512]{1,0:T(8,128)S(1)} collective-permute-done((f32[16,512]{1,0:T(8,128)S(1)}, f32[16,512]{1,0:T(8,128)S(1)}, u32[]{:S(2)}, u32[]{:S(2)}) %collective-permute-start) | collective-permute-done | bytes 32800 | tf_op jit(solution)/shard_map/while/body/eval_jaxpr/ppermute | solution.py:13
  940.2 15.1 %collective-permute-done = f32[16,512]{1,0:T(8,128)S(1)} collective-permute-done((f32[16,512]{1,0:T(8,128)S(1)}, f32[16,512]{1,0:T(8,128)S(1)}, u32[]{:S(2)}, u32[]{:S(2)}) %collective-permute-start) | collective-permute-done | bytes 32800 | tf_op jit(solution)/shard_map/while/body/eval_jaxpr/ppermute | solution.py:13
  974.2 15.1 %collective-permute-done = f32[16,512]{1,0:T(8,128)S(1)} collective-permute-done((f32[16,512]{1,0:T(8,128)S(1)}, f32[16,512]{1,0:T(8,128)S(1)}, u32[]{:S(2)}, u32[]{:S(2)}) %collective-permute-start) | collective-permute-done | bytes 32800 | tf_op jit(solution)/shard_map/while/body/eval_jaxpr/ppermute | solution.py:13
  1144.3 15.1 %collective-permute-done = f32[16,512]{1,0:T(8,128)S(1)} collective-permute-done((f32[16,512]{1,0:T(8,128)S(1)}, f32[16,512]{1,0:T(8,128)S(1)}, u32[]{:S(2)}, u32[]{:S(2)}) %collective-permute-start) | collective-permute-done | bytes 32800 | tf_op jit(solution)/shard_map/while/body/eval_jaxpr/ppermute | solution.py:13
  1178.3 15.1 %collective-permute-done = f32[16,512]{1,0:T(8,128)S(1)} collective-permute-done((f32[16,512]{1,0:T(8,128)S(1)}, f32[16,512]{1,0:T(8,128)S(1)}, u32[]{:S(2)}, u32[]{:S(2)}) %collective-permute-start) | collective-permute-done | bytes 32800 | tf_op jit(solution)/shard_map/while/body/eval_jaxpr/ppermute | solution.py:13
  (201 shorter events, 800.5 us)
Async XLA Ops:
  6.5 65.0 %all-gather.3.cloned.1.call-start = ((), (), s32[]{:S(2)}) async-start(), calls=%async_computation | async-start | bytes 2359296 | tf_op jit(solution)/shard_map/all_gather | solution.py:82
  7.3 289.7 %all-gather.5.cloned.1.call-start = ((), (), s32[]{:S(2)}) async-start(), calls=%async_computation.1 | async-start | bytes 12779520 | tf_op jit(solution)/shard_map/all_gather | solution.py:87
  324.7 17.1 %collective-permute-start = (f32[16,512]{1,0:T(8,128)S(1)}, f32[16,512]{1,0:T(8,128)S(1)}, u32[]{:S(2)}, u32[]{:S(2)}) collective-permute-start(f32[16,512]{1,0:T(8,128)S(1)} %multiply_add_fusion.5), channel_id=1, source_target_pairs={{0,8},{8,16},{16,24},{24,32},{32,40},{40,48},{48,56},{56,64},{64,7... | collective-permute-start | bytes 98312 | tf_op jit(solution)/shard_map/while/body/eval_jaxpr/ppermute | solution.py:13
  375.8 17.2 %collective-permute-start = (f32[16,512]{1,0:T(8,128)S(1)}, f32[16,512]{1,0:T(8,128)S(1)}, u32[]{:S(2)}, u32[]{:S(2)}) collective-permute-start(f32[16,512]{1,0:T(8,128)S(1)} %multiply_add_fusion.5), channel_id=1, source_target_pairs={{0,8},{8,16},{16,24},{24,32},{32,40},{40,48},{48,56},{56,64},{64,7... | collective-permute-start | bytes 98312 | tf_op jit(solution)/shard_map/while/body/eval_jaxpr/ppermute | solution.py:13
  393.0 17.5 %collective-permute-start = (f32[16,512]{1,0:T(8,128)S(1)}, f32[16,512]{1,0:T(8,128)S(1)}, u32[]{:S(2)}, u32[]{:S(2)}) collective-permute-start(f32[16,512]{1,0:T(8,128)S(1)} %multiply_add_fusion.5), channel_id=1, source_target_pairs={{0,8},{8,16},{16,24},{24,32},{32,40},{40,48},{48,56},{56,64},{64,7... | collective-permute-start | bytes 98312 | tf_op jit(solution)/shard_map/while/body/eval_jaxpr/ppermute | solution.py:13
  410.4 17.4 %collective-permute-start = (f32[16,512]{1,0:T(8,128)S(1)}, f32[16,512]{1,0:T(8,128)S(1)}, u32[]{:S(2)}, u32[]{:S(2)}) collective-permute-start(f32[16,512]{1,0:T(8,128)S(1)} %multiply_add_fusion.5), channel_id=1, source_target_pairs={{0,8},{8,16},{16,24},{24,32},{32,40},{40,48},{48,56},{56,64},{64,7... | collective-permute-start | bytes 98312 | tf_op jit(solution)/shard_map/while/body/eval_jaxpr/ppermute | solution.py:13
  444.8 17.1 %collective-permute-start = (f32[16,512]{1,0:T(8,128)S(1)}, f32[16,512]{1,0:T(8,128)S(1)}, u32[]{:S(2)}, u32[]{:S(2)}) collective-permute-start(f32[16,512]{1,0:T(8,128)S(1)} %multiply_add_fusion.5), channel_id=1, source_target_pairs={{0,8},{8,16},{16,24},{24,32},{32,40},{40,48},{48,56},{56,64},{64,7... | collective-permute-start | bytes 98312 | tf_op jit(solution)/shard_map/while/body/eval_jaxpr/ppermute | solution.py:13
  461.9 17.2 %collective-permute-start = (f32[16,512]{1,0:T(8,128)S(1)}, f32[16,512]{1,0:T(8,128)S(1)}, u32[]{:S(2)}, u32[]{:S(2)}) collective-permute-start(f32[16,512]{1,0:T(8,128)S(1)} %multiply_add_fusion.5), channel_id=1, source_target_pairs={{0,8},{8,16},{16,24},{24,32},{32,40},{40,48},{48,56},{56,64},{64,7... | collective-permute-start | bytes 98312 | tf_op jit(solution)/shard_map/while/body/eval_jaxpr/ppermute | solution.py:13
  496.1 17.0 %collective-permute-start = (f32[16,512]{1,0:T(8,128)S(1)}, f32[16,512]{1,0:T(8,128)S(1)}, u32[]{:S(2)}, u32[]{:S(2)}) collective-permute-start(f32[16,512]{1,0:T(8,128)S(1)} %multiply_add_fusion.5), channel_id=1, source_target_pairs={{0,8},{8,16},{16,24},{24,32},{32,40},{40,48},{48,56},{56,64},{64,7... | collective-permute-start | bytes 98312 | tf_op jit(solution)/shard_map/while/body/eval_jaxpr/ppermute | solution.py:13
  530.1 17.0 %collective-permute-start = (f32[16,512]{1,0:T(8,128)S(1)}, f32[16,512]{1,0:T(8,128)S(1)}, u32[]{:S(2)}, u32[]{:S(2)}) collective-permute-start(f32[16,512]{1,0:T(8,128)S(1)} %multiply_add_fusion.5), channel_id=1, source_target_pairs={{0,8},{8,16},{16,24},{24,32},{32,40},{40,48},{48,56},{56,64},{64,7... | collective-permute-start | bytes 98312 | tf_op jit(solution)/shard_map/while/body/eval_jaxpr/ppermute | solution.py:13
  564.1 17.0 %collective-permute-start = (f32[16,512]{1,0:T(8,128)S(1)}, f32[16,512]{1,0:T(8,128)S(1)}, u32[]{:S(2)}, u32[]{:S(2)}) collective-permute-start(f32[16,512]{1,0:T(8,128)S(1)} %multiply_add_fusion.5), channel_id=1, source_target_pairs={{0,8},{8,16},{16,24},{24,32},{32,40},{40,48},{48,56},{56,64},{64,7... | collective-permute-start | bytes 98312 | tf_op jit(solution)/shard_map/while/body/eval_jaxpr/ppermute | solution.py:13
  598.1 17.0 %collective-permute-start = (f32[16,512]{1,0:T(8,128)S(1)}, f32[16,512]{1,0:T(8,128)S(1)}, u32[]{:S(2)}, u32[]{:S(2)}) collective-permute-start(f32[16,512]{1,0:T(8,128)S(1)} %multiply_add_fusion.5), channel_id=1, source_target_pairs={{0,8},{8,16},{16,24},{24,32},{32,40},{40,48},{48,56},{56,64},{64,7... | collective-permute-start | bytes 98312 | tf_op jit(solution)/shard_map/while/body/eval_jaxpr/ppermute | solution.py:13
  632.1 17.0 %collective-permute-start = (f32[16,512]{1,0:T(8,128)S(1)}, f32[16,512]{1,0:T(8,128)S(1)}, u32[]{:S(2)}, u32[]{:S(2)}) collective-permute-start(f32[16,512]{1,0:T(8,128)S(1)} %multiply_add_fusion.5), channel_id=1, source_target_pairs={{0,8},{8,16},{16,24},{24,32},{32,40},{40,48},{48,56},{56,64},{64,7... | collective-permute-start | bytes 98312 | tf_op jit(solution)/shard_map/while/body/eval_jaxpr/ppermute | solution.py:13
  666.1 17.0 %collective-permute-start = (f32[16,512]{1,0:T(8,128)S(1)}, f32[16,512]{1,0:T(8,128)S(1)}, u32[]{:S(2)}, u32[]{:S(2)}) collective-permute-start(f32[16,512]{1,0:T(8,128)S(1)} %multiply_add_fusion.5), channel_id=1, source_target_pairs={{0,8},{8,16},{16,24},{24,32},{32,40},{40,48},{48,56},{56,64},{64,7... | collective-permute-start | bytes 98312 | tf_op jit(solution)/shard_map/while/body/eval_jaxpr/ppermute | solution.py:13
  734.2 17.0 %collective-permute-start = (f32[16,512]{1,0:T(8,128)S(1)}, f32[16,512]{1,0:T(8,128)S(1)}, u32[]{:S(2)}, u32[]{:S(2)}) collective-permute-start(f32[16,512]{1,0:T(8,128)S(1)} %multiply_add_fusion.5), channel_id=1, source_target_pairs={{0,8},{8,16},{16,24},{24,32},{32,40},{40,48},{48,56},{56,64},{64,7... | collective-permute-start | bytes 98312 | tf_op jit(solution)/shard_map/while/body/eval_jaxpr/ppermute | solution.py:13
  768.2 17.0 %collective-permute-start = (f32[16,512]{1,0:T(8,128)S(1)}, f32[16,512]{1,0:T(8,128)S(1)}, u32[]{:S(2)}, u32[]{:S(2)}) collective-permute-start(f32[16,512]{1,0:T(8,128)S(1)} %multiply_add_fusion.5), channel_id=1, source_target_pairs={{0,8},{8,16},{16,24},{24,32},{32,40},{40,48},{48,56},{56,64},{64,7... | collective-permute-start | bytes 98312 | tf_op jit(solution)/shard_map/while/body/eval_jaxpr/ppermute | solution.py:13
  802.2 17.0 %collective-permute-start = (f32[16,512]{1,0:T(8,128)S(1)}, f32[16,512]{1,0:T(8,128)S(1)}, u32[]{:S(2)}, u32[]{:S(2)}) collective-permute-start(f32[16,512]{1,0:T(8,128)S(1)} %multiply_add_fusion.5), channel_id=1, source_target_pairs={{0,8},{8,16},{16,24},{24,32},{32,40},{40,48},{48,56},{56,64},{64,7... | collective-permute-start | bytes 98312 | tf_op jit(solution)/shard_map/while/body/eval_jaxpr/ppermute | solution.py:13
  938.2 17.0 %collective-permute-start = (f32[16,512]{1,0:T(8,128)S(1)}, f32[16,512]{1,0:T(8,128)S(1)}, u32[]{:S(2)}, u32[]{:S(2)}) collective-permute-start(f32[16,512]{1,0:T(8,128)S(1)} %multiply_add_fusion.5), channel_id=1, source_target_pairs={{0,8},{8,16},{16,24},{24,32},{32,40},{40,48},{48,56},{56,64},{64,7... | collective-permute-start | bytes 98312 | tf_op jit(solution)/shard_map/while/body/eval_jaxpr/ppermute | solution.py:13
  972.3 17.0 %collective-permute-start = (f32[16,512]{1,0:T(8,128)S(1)}, f32[16,512]{1,0:T(8,128)S(1)}, u32[]{:S(2)}, u32[]{:S(2)}) collective-permute-start(f32[16,512]{1,0:T(8,128)S(1)} %multiply_add_fusion.5), channel_id=1, source_target_pairs={{0,8},{8,16},{16,24},{24,32},{32,40},{40,48},{48,56},{56,64},{64,7... | collective-permute-start | bytes 98312 | tf_op jit(solution)/shard_map/while/body/eval_jaxpr/ppermute | solution.py:13
  1006.3 17.0 %collective-permute-start = (f32[16,512]{1,0:T(8,128)S(1)}, f32[16,512]{1,0:T(8,128)S(1)}, u32[]{:S(2)}, u32[]{:S(2)}) collective-permute-start(f32[16,512]{1,0:T(8,128)S(1)} %multiply_add_fusion.5), channel_id=1, source_target_pairs={{0,8},{8,16},{16,24},{24,32},{32,40},{40,48},{48,56},{56,64},{64,7... | collective-permute-start | bytes 98312 | tf_op jit(solution)/shard_map/while/body/eval_jaxpr/ppermute | solution.py:13
  1142.3 17.0 %collective-permute-start = (f32[16,512]{1,0:T(8,128)S(1)}, f32[16,512]{1,0:T(8,128)S(1)}, u32[]{:S(2)}, u32[]{:S(2)}) collective-permute-start(f32[16,512]{1,0:T(8,128)S(1)} %multiply_add_fusion.5), channel_id=1, source_target_pairs={{0,8},{8,16},{16,24},{24,32},{32,40},{40,48},{48,56},{56,64},{64,7... | collective-permute-start | bytes 98312 | tf_op jit(solution)/shard_map/while/body/eval_jaxpr/ppermute | solution.py:13
  1176.4 17.0 %collective-permute-start = (f32[16,512]{1,0:T(8,128)S(1)}, f32[16,512]{1,0:T(8,128)S(1)}, u32[]{:S(2)}, u32[]{:S(2)}) collective-permute-start(f32[16,512]{1,0:T(8,128)S(1)} %multiply_add_fusion.5), channel_id=1, source_target_pairs={{0,8},{8,16},{16,24},{24,32},{32,40},{40,48},{48,56},{56,64},{64,7... | collective-permute-start | bytes 98312 | tf_op jit(solution)/shard_map/while/body/eval_jaxpr/ppermute | solution.py:13
  1210.4 17.0 %collective-permute-start = (f32[16,512]{1,0:T(8,128)S(1)}, f32[16,512]{1,0:T(8,128)S(1)}, u32[]{:S(2)}, u32[]{:S(2)}) collective-permute-start(f32[16,512]{1,0:T(8,128)S(1)} %multiply_add_fusion.5), channel_id=1, source_target_pairs={{0,8},{8,16},{16,24},{24,32},{32,40},{40,48},{48,56},{56,64},{64,7... | collective-permute-start | bytes 98312 | tf_op jit(solution)/shard_map/while/body/eval_jaxpr/ppermute | solution.py:13
  1244.4 17.0 %collective-permute-start = (f32[16,512]{1,0:T(8,128)S(1)}, f32[16,512]{1,0:T(8,128)S(1)}, u32[]{:S(2)}, u32[]{:S(2)}) collective-permute-start(f32[16,512]{1,0:T(8,128)S(1)} %multiply_add_fusion.5), channel_id=1, source_target_pairs={{0,8},{8,16},{16,24},{24,32},{32,40},{40,48},{48,56},{56,64},{64,7... | collective-permute-start | bytes 98312 | tf_op jit(solution)/shard_map/while/body/eval_jaxpr/ppermute | solution.py:13
  (44 other events, 1788.8 us)
Sparse Core Ops, SparseCore 0:
  9.4 62.0 all-gather.2
  75.9 220.9 all-gather.4
where the time goes:
time: 1420 us
  waiting for transfers between devices  1250 us (88%)
  starting transfers between devices  123 us (9%)
  matrix products  23 us (2%)
    ppermute x64, waiting for transfers between devices, from_behind(): return lax.ppermute(value, axis, pairs)  965 us
    all_gather x1, waiting for transfers between devices, local(): lax.all_gather(w_in, 'seq', axis=0, tiled=True)  225 us
    ppermute x64, starting transfers between devices, from_behind(): return lax.ppermute(value, axis, pairs)  123 us
    all_gather x1, waiting for transfers between devices, local(): whole = lax.all_gather(tokens, 'chan', axis=1, tiled=True)  59.9 us
  transfers between devices with their start and end apart: 66, of which 66 were waited for; matrix products, arithmetic and copies ran while one was open for 0% of the time, Pallas kernels for 0%

commit v1 on v0

v1 whole, which is shorter than its diff:
```python
import jax
import jax.numpy as jnp
from jax import lax
from jax.experimental import pallas as pl
from jax.experimental.pallas import tpu as pltpu
from jax.sharding import PartitionSpec as P

MESH = pl.DeviceIdType.MESH
F32, BF16 = jnp.float32, jnp.bfloat16
ROWS = 256
CH = 512
DEPTH = 64
MODES = 16
SEQ = 16384.0
SUBS = 8
STEPS = ROWS // SUBS
COPIES = 112


def rounded(value):
    return value.astype(BF16).astype(F32)


def kernel(
    tok, w, taps, res, poles, skip, out,
    wbuf, xbuf, acc, legs, gbuf, ybuf, qbuf, obuf, ends, prefix, decay, tail_w, head_w, powers,
    state, sib_state, c_msg, y_in, r_msg, x_in, z_msg, z_in, k_msg, k_in, carry, halo_out, halo_in,
    send, recv, loc,
):
    s, c = lax.axis_index("seq"), lax.axis_index("chan")
    k, zh = lax.rem(s, 2), lax.rem(lax.div(s, 2), 2)
    y, x = lax.rem(lax.div(s, 4), 4), lax.div(s, 16)

    def at(px=x, py=y, pzh=zh, pk=k, pc=c):
        return (((px * 4 + py) * 2 + pzh) * 2 + pk, pc)

    def xs(d):
        return lax.rem(x + d + 4, 4)

    def ys(d):
        return lax.rem(y + d + 4, 4)

    over = lax.div(c + 4, 8)
    far_c = lax.rem(c + 4, 8)
    z_up = at(pzh=lax.rem(zh + over, 2), pc=far_c)
    z_dn = at(pzh=lax.rem(zh + over + 1, 2), pc=far_c)
    sibling = at(pk=1 - k)
    opposite = at(pzh=1 - zh)
    up, dn = lax.rem(c + 1, 8), lax.rem(c + 7, 8)
    after, before = (lax.rem(s + 1, 64), c), (lax.rem(s + 63, 64), c)

    barrier = pltpu.get_barrier_semaphore()
    partners = [sibling, opposite, z_up, z_dn, (s, up), (s, dn), after, before]
    for d in (1, 2, 3):
        partners += [at(px=xs(d)), at(py=ys(d))]
    for partner in partners:
        pl.semaphore_signal(barrier, inc=1, device_id=partner, device_id_type=MESH)
    pl.semaphore_wait(barrier, len(partners))

    sent = []

    def start(src, dst, to, cond=None):
        i = len(sent)
        copy = pltpu.make_async_remote_copy(
            src_ref=src, dst_ref=dst, send_sem=send.at[i], recv_sem=recv.at[i],
            device_id=to, device_id_type=MESH,
        )
        if cond is None:
            copy.start()
        else:
            pl.when(cond)(lambda: copy.start())
        sent.append((copy, cond))
        return copy

    chain = {}

    def tok_send(j, h):
        rows = pl.ds(h * 128, 128)
        low, high = lax.rem(c - j + 9, 8), lax.rem(c + j - 1, 8)
        for way, block, to, cond in (
            (0, low, up, (c < 7) & (c >= j - 1)),
            (1, high, dn, (c > 0) & (c + j <= 8)),
        ):
            src = tok.at[rows] if j == 1 else xbuf.at[block, rows]
            chain[j, h, way] = start(src, xbuf.at[block, rows], (s, to), cond)

    def tok_step(j, h):
        pl.when(c >= j)(lambda: chain[j, h, 0].wait_recv())
        pl.when(c + j <= 7)(lambda: chain[j, h, 1].wait_recv())
        if j < 7:
            tok_send(j + 1, h)

    def one(which, d, zz, rows):
        px, py = (xs(d), y) if which == "x" else (x, ys(d))
        return wbuf.at[px, py, zz, k, rows]

    def line(which, d, zz, rows):
        if which == "x":
            return wbuf.at[xs(d), pl.ds(0, 4), zz, k, rows]
        return wbuf.at[pl.ds(0, 4), ys(d), zz, k, rows]

    def to(which, d):
        return at(px=xs(d)) if which == "x" else at(py=ys(d))

    ORDER = (("x", "y", 0), ("y", "x", 32))

    class Gather:
        def __init__(self, zz, own):
            self.zz = zz
            self.sib = []
            self.near = {}
            for first, _, r in ORDER:
                rows = pl.ds(r, 32)
                src = w.at[rows] if own else one(first, 0, zz, rows)
                for d in (1, -1):
                    self.near[first, d] = start(src, one(first, 0, zz, rows), to(first, d))

        def pass_on(self):
            self.far = []
            for first, _, r in ORDER:
                for d in (1, -1):
                    rows = pl.ds(r + (0 if d == 1 else 16), 16)
                    self.near[first, d].wait_recv()
                    self.far.append(start(one(first, -d, self.zz, rows), one(first, -d, self.zz, rows), to(first, d)))

        def turn(self):
            for copy in self.far:
                copy.wait_recv()
            self.near2 = {}
            for _, second, r in ORDER:
                ref = line(second, 0, self.zz, pl.ds(r, 32))
                for d in (1, -1):
                    self.near2[second, d] = start(ref, ref, to(second, d))
            for _, second, r in ORDER:
                ref = line(second, 0, self.zz, pl.ds(r, 32))
                self.sib.append(start(ref, ref, sibling))

        def pass_on2(self):
            self.far2 = []
            for _, second, r in ORDER:
                for d in (1, -1):
                    rows = pl.ds(r + (0 if d == 1 else 16), 16)
                    self.near2[second, d].wait_recv()
                    ref = line(second, -d, self.zz, rows)
                    self.far2.append(start(ref, ref, to(second, d)))
            for _, second, r in ORDER:
                for d in (1, -1):
                    ref = line(second, d, self.zz, pl.ds(r, 32))
                    self.sib.append(start(ref, ref, sibling))

        def finish(self):
            for copy in self.far2:
                copy.wait_recv()
            for _, second, r in ORDER:
                ref = line(second, 2, self.zz, pl.ds(r, 32))
                self.sib.append(start(ref, ref, sibling))

        def wait_sibling(self):
            for copy in self.sib:
                copy.wait_recv()

    leg_a = start(w.at[pl.ds(0, 32)], legs.at[0], z_up)
    leg_b = start(w.at[pl.ds(32, 32)], legs.at[1], z_dn)
    tok_send(1, 0)
    tok_send(1, 1)
    mine = Gather(zh, True)
    keep_w = pltpu.make_async_copy(w, wbuf.at[x, y, zh, k], loc.at[0])
    keep_x = pltpu.make_async_copy(tok, xbuf.at[c], loc.at[1])
    keep_w.start()
    keep_x.start()

    def tables():
        acc[...] = jnp.zeros_like(acc)
        rate = poles[...] * (-1.0 / SEQ)
        decay[...] = jnp.exp(rate)
        powers[0] = jnp.exp(rate * ROWS)
        powers[1] = jnp.exp(rate * (2.0 * ROWS))
        powers[2] = jnp.exp(rate * (4.0 * ROWS))
        powers[3] = jnp.exp(rate * (16.0 * ROWS))
        powers[4] = jnp.exp(rate * ((4.0 * ROWS) * y.astype(F32)))
        powers[5] = jnp.exp(rate * (STEPS - 1.0))
        powers[6] = jnp.exp(rate * (STEPS - 2.0))
        sub = lax.broadcasted_iota(jnp.int32, (SUBS, CH), 0).astype(F32)
        for n in range(MODES):
            r = poles[n : n + 1, :] * (-STEPS / SEQ)
            head_w[n] = jnp.exp(r * sub)
            tail_w[n] = jnp.exp(r * (SUBS - 1.0 - sub))

    tok_step(1, 0)
    mine.pass_on()
    tok_step(1, 1)
    keep_w.wait()
    mine.turn()
    tables()
    tok_step(2, 0)
    leg_a.wait_recv()
    leg_c = start(legs.at[0], wbuf.at[x, y, 1 - z_up_zh(zh, over), k, pl.ds(0, 32)], z_up)
    leg_b.wait_recv()
    leg_d = start(legs.at[1], wbuf.at[x, y, z_up_zh(zh, over), k, pl.ds(32, 32)], z_dn)
    tok_step(2, 1)
    mine.pass_on2()
    tok_step(3, 0)
    tok_step(3, 1)
    mine.finish()
    leg_c.wait_recv()
    leg_d.wait_recv()
    theirs = Gather(1 - zh, False)
    tok_step(4, 0)
    theirs.pass_on()
    tok_step(4, 1)
    theirs.turn()
    tok_step(5, 0)
    tok_step(5, 1)
    theirs.pass_on2()
    tok_step(6, 0)
    mine.wait_sibling()
    tok_step(6, 1)
    theirs.finish()
    keep_x.wait()
    theirs.wait_sibling()

    def dot_chunk(cc):
        px, py = lax.div(cc, 2), lax.rem(cc, 2) * 2
        for g in range(3):
            cols = pl.ds(g * CH, CH)
            part = wbuf[px, pl.ds(py, 2), :, :, :, cols].reshape(CH, CH)
            dot = jnp.dot(xbuf[cc], part, preferred_element_type=F32)
            for lg in range(4):
                acc[4 * g + lg, 8:, :] += dot[:, lg * 128 : (lg + 1) * 128]

    def dots(lo, hi):
        def body(j, _):
            pl.when(c >= j)(lambda: dot_chunk(lax.rem(c - j + 8, 8)))
            pl.when((j > 0) & (c + j <= 7))(lambda: dot_chunk(lax.rem(c + j, 8)))
            return 0

        lax.fori_loop(lo, hi, body, 0)

    dots(0, 7)
    tok_step(7, 0)
    tok_step(7, 1)
    dots(7, 8)

    for r in range(2):
        for i in range(12):
            row, cols = 3 * r + i // 4, (i % 4) * 128
            halo_out[row : row + 1, cols : cols + 128] = rounded(acc[i, 6 + ROWS + r : 7 + ROWS + r, :])
    halo = start(halo_out, halo_in, after, s < 63)

    def lanes(lg):
        return pl.ds(lg * 128, 128)

    def rows_of(ref, lg):
        return [jnp.broadcast_to(ref[n : n + 1, lanes(lg)], (SUBS, 128)) for n in range(MODES)]

    def filter_of(g, lg):
        t = [jnp.broadcast_to(taps[i, g : g + 1, lanes(lg)], (SUBS, 128)) for i in range(3)]

        def load(first):
            return rounded(acc[4 * g + lg, pl.ds(first, SUBS, stride=STEPS), :])

        return lambda p0, p1, p2: t[0] * p0 + t[1] * p1 + t[2] * p2, load

    def gate(fk, fv, k3, v3):
        return rounded(fk(*k3) * fv(*v3))

    def pass_a(lg):
        (fk, lk), (fv, lv) = filter_of(1, lg), filter_of(2, lg)
        a = rows_of(decay, lg)

        def body(i, held):
            k1, k2, v1, v2, st = held
            k0, v0 = lk(8 + i), lv(8 + i)
            g = gate(fk, fv, (k0, k1, k2), (v0, v1, v2))
            gbuf[i, :, lanes(lg)] = g
            return k0, k1, v0, v1, tuple(a[n] * st[n] + g for n in range(MODES))

        zero = tuple(jnp.zeros((SUBS, 128), F32) for _ in range(MODES))
        held = lax.fori_loop(0, STEPS, body, (lk(7), lk(6), lv(7), lv(6), zero), unroll=4)
        for n in range(MODES):
            ends[n, :, lanes(lg)] = held[4][n]

    for lg in range(4):
        pass_a(lg)

    @pl.when(s > 0)
    def _():
        halo.wait_recv()
        for r in range(2):
            for i in range(12):
                row, cols = 3 * r + i // 4, (i % 4) * 128
                acc[i, 6 + r : 7 + r, :] = halo_in[row : row + 1, cols : cols + 128]

    for lg in range(4):
        (fk, lk), (fv, lv) = filter_of(1, lg), filter_of(2, lg)
        pk, pv = [lk(6 + i) for i in range(4)], [lv(6 + i) for i in range(4)]
        g0 = gate(fk, fv, pk[2::-1], pv[2::-1])
        g1 = gate(fk, fv, pk[3:0:-1], pv[3:0:-1])
        d0, d1 = g0 - gbuf[0, :, lanes(lg)], g1 - gbuf[1, :, lanes(lg)]
        gbuf[0, :, lanes(lg)] = g0
        gbuf[1, :, lanes(lg)] = g1
        for n in range(MODES):
            end = ends[n, :, lanes(lg)] + powers[5, n : n + 1, lanes(lg)] * d0 + powers[6, n : n + 1, lanes(lg)] * d1
            ends[n, :, lanes(lg)] = end
            state[n : n + 1, lanes(lg)] = jnp.sum(tail_w[n, :, lanes(lg)] * end, axis=0, keepdims=True)

    def pass_b(lg):
        fq, lq = filter_of(0, lg)
        a, r = rows_of(decay, lg), rows_of(res, lg)
        gain = jnp.broadcast_to(skip[0:1, lanes(lg)], (SUBS, 128))

        def body(i, held):
            q1, q2, st = held
            q0 = lq(8 + i)
            qbuf[i, :, lanes(lg)] = fq(q0, q1, q2)
            g = gbuf[i, :, lanes(lg)]
            st = tuple(a[n] * st[n] + g for n in range(MODES))
            ybuf[i, :, lanes(lg)] = total([r[n] * st[n] for n in range(MODES)] + [gain * g])
            return q0, q1, st

        zero = tuple(jnp.zeros((SUBS, 128), F32) for _ in range(MODES))
        lax.fori_loop(0, STEPS, body, (lq(7), lq(6), zero), unroll=2)
        sub = lax.broadcasted_iota(jnp.int32, (SUBS, 128), 0)

        def down(value, by):
            return jnp.where(sub >= by, pltpu.roll(value, by, 0), 0.0)

        for n in range(MODES):
            v = down(ends[n, :, lanes(lg)], 1)
            for by in (1, 2, 4):
                v = v + head_w[n, by : by + 1, lanes(lg)] * down(v, by)
            prefix[n, :, lanes(lg)] = v

    half = pl.ds(pl.multiple_of(k * 256, 256), 256)
    other = pl.ds(pl.multiple_of((1 - k) * 256, 256), 256)
    first = start(state, sib_state, sibling)
    pass_b(0)
    first.wait_recv()
    own, sib = state[:, half], sib_state[:, half]
    chip = powers[0, :, half] * jnp.where(k == 0, own, sib) + jnp.where(k == 0, sib, own)
    c_msg[...] = chip
    y_in[y] = chip
    level = [start(c_msg, y_in.at[y], at(py=ys(d))) for d in (1, 2, 3)]
    pass_b(1)
    for copy in level:
        copy.wait_recv()
    d4 = powers[2, :, half]
    row, early = jnp.zeros_like(chip), jnp.zeros_like(chip)
    for i in range(4):
        got = y_in[i]
        row = row * d4 + got
        early = jnp.where(i < y, early * d4 + got, early)
    r_msg[...] = row
    x_in[x] = row
    level = [start(r_msg, x_in.at[x], at(px=xs(d))) for d in (1, 2, 3)]
    pass_b(2)
    for copy in level:
        copy.wait_recv()
    d16, lead = powers[3, :, half], jnp.zeros_like(chip)
    for i in range(4):
        lead = jnp.where(i < x, lead * d16 + x_in[i], lead)
    plane = early + powers[4, :, half] * lead
    z_msg[...] = jnp.where(zh == 0, d4 * plane + chip, plane)
    level = start(z_msg, z_in, opposite)
    pass_b(3)
    level.wait_recv()
    into = powers[1, :, half] * plane + z_in[...]
    k_msg[...] = into
    level = start(k_msg, k_in, sibling)
    carry[:, half] = into
    level.wait_recv()
    carry[:, other] = k_in[...]
    carry[...] = jnp.where(k == 0, carry[...], powers[0] * carry[...] + sib_state[...])

    def pass_c(lg):
        a, r = rows_of(decay, lg), rows_of(res, lg)
        ws = tuple(
            r[n] * (prefix[n, :, lanes(lg)] + head_w[n, :, lanes(lg)] * carry[n : n + 1, lanes(lg)])
            for n in range(MODES)
        )

        def body(i, ws):
            ws = tuple(a[n] * ws[n] for n in range(MODES))
            value = ybuf[i, :, lanes(lg)] + total(list(ws))
            obuf[lg, pl.ds(i, SUBS, stride=STEPS), :] = qbuf[i, :, lanes(lg)] * value
            return ws

        lax.fori_loop(0, STEPS, body, ws, unroll=4)
        out[:, lanes(lg)] = obuf[lg].astype(BF16)

    for lg in range(4):
        pass_c(lg)

    for copy, cond in sent:
        if cond is None:
            copy.wait_send()
        else:
            pl.when(cond)(lambda copy=copy: copy.wait_send())


def z_up_zh(zh, over):
    return lax.rem(zh + over, 2)


def total(values):
    while len(values) > 1:
        values = [a + b for a, b in zip(values[::2], values[1::2])] + values[len(values) & ~1 :]
    return values[0]


def local(tokens, w_in, short_taps, residues, poles, skip_gain):
    vmem = pl.BlockSpec(memory_space=pltpu.VMEM)
    block = pltpu.VMEM((STEPS, SUBS, CH), F32)
    table = pltpu.VMEM((MODES, SUBS, CH), F32)
    full, part = pltpu.VMEM((MODES, CH), F32), pltpu.VMEM((MODES, CH // 2), F32)
    parts4 = pltpu.VMEM((4, MODES, CH // 2), F32)
    halo = pltpu.VMEM((8, CH), F32)
    return pl.pallas_call(
        kernel,
        out_shape=jax.ShapeDtypeStruct((ROWS, CH), BF16),
        in_specs=[vmem] * 6,
        out_specs=vmem,
        scratch_shapes=[
            pltpu.VMEM((4, 4, 2, 2, DEPTH, 3 * CH), BF16),
            pltpu.VMEM((8, ROWS, CH), BF16),
            pltpu.VMEM((12, 8 + ROWS, 128), F32),
            pltpu.VMEM((2, DEPTH // 2, 3 * CH), BF16),
            block, block, block,
            pltpu.VMEM((4, ROWS, 128), F32),
            table, table, full, table, table,
            pltpu.VMEM((7, MODES, CH), F32),
            full, full, part, parts4, part, parts4, part, part, part, part, full, halo, halo,
            pltpu.SemaphoreType.DMA((COPIES,)),
            pltpu.SemaphoreType.DMA((COPIES,)),
            pltpu.SemaphoreType.DMA((2,)),
        ],
        compiler_params=pltpu.CompilerParams(
            collective_id=0, has_side_effects=True, vmem_limit_bytes=40 * 1024 * 1024
        ),
    )(tokens, w_in.reshape(DEPTH, 3 * CH), short_taps, residues, poles, skip_gain.reshape(1, CH))


def solution(mesh):
    placed = (
        P("seq", "chan"),
        P("seq", None, "chan"),
        P(None, None, "chan"),
        P(None, "chan"),
        P(None, "chan"),
        P("chan"),
    )
    return jax.shard_map(
        local, mesh=mesh, in_specs=placed, out_specs=P("seq", "chan"), check_vma=False
    )
```

time: 1420 us -> 112 us (0.08)
  the two profiles are of different devices: /device:TPU:100 before, /device:TPU:1 now
where the time goes in v1:
time: 112 us
  Pallas kernels  110 us (98%)
  local copies, waits for them, and re-layouts  1.73 us (2%)
    pallas_call x1, Pallas kernels, local(): pl.pallas_call(kernel, out_shape=jax.ShapeDtypeStruct((ROWS, CH), BF16),...  110 us

profile of v1, /device:TPU:1, one launch (start us, length us, event | category | flops | bytes accessed | tf_op | source)
XLA Modules:
  0.0 112.1 jit_solution(18358871328528241535)
XLA Ops:
  0.0 0.0 copy-start
  0.0 0.0 copy-start.1
  0.0 0.0 copy-start.2
  0.0 0.0 copy-start.3
  0.0 0.0 copy-start.4
  0.0 1.0 copy.9
  1.0 0.0 copy-done
  1.0 0.0 copy-done.1
  1.0 0.0 copy-done.2
  1.1 0.0 copy-done.3
  1.1 0.0 copy-done.4
  1.1 110.4 %shard_map.64 = bf16[256,512]{1,0:T(8,128)(2,1)S(1)} custom-call(bf16[256,512]{1,0:T(8,128)(2,1)S(1)} %copy-done, bf16[64,1536]{1,0:T(8,128)(2,1)S(1)} %bitcast.3, f32[3,3,512]{2,1,0:T(4,128)S(1)} %copy-done.3, f32[16,512]{1,0:T(8,128)S(1)} %copy-done.1, f32[16,512]{1,0:T(8,128)S(1)} %copy-done.2, f32[1,512]{1,0:T(1,128)S(1)} %bitcast.4), custom_call_target="tpu_custom_call" | custom-call | tf_op jit(solution)/shard_map/pallas_call | solution.py:418
  111.4 0.7 copy.11
Async XLA Ops:
  0.0 1.0 copy-start
  0.0 1.0 copy-start.1
  0.0 1.0 copy-start.2
  0.0 1.0 copy-start.3
  0.0 1.0 copy-start.4

commit v2 on v1

--- a/solution.py
+++ b/solution.py
@@ -14,7 +14,8 @@
 SEQ = 16384.0
 SUBS = 8
 STEPS = ROWS // SUBS
-COPIES = 112
+TOP = 16
+COPIES = 176
 
 
 def rounded(value):
@@ -24,7 +25,7 @@
 def kernel(
     tok, w, taps, res, poles, skip, out,
     wbuf, xbuf, acc, legs, gbuf, ybuf, qbuf, obuf, ends, prefix, decay, tail_w, head_w, powers,
-    state, sib_state, c_msg, y_in, r_msg, x_in, z_msg, z_in, k_msg, k_in, carry, halo_out, halo_in,
+    state, sib_state, c_msg, y_in, r_msg, x_in, z_msg, z_in, k_msg, k_in, carry, packed, last_out, last_in, last,
     send, recv, loc,
 ):
     s, c = lax.axis_index("seq"), lax.axis_index("chan")
@@ -74,21 +75,33 @@
 
     chain = {}
 
-    def tok_send(j, h):
-        rows = pl.ds(h * 128, 128)
+    def pass_along(j, key, ref):
         low, high = lax.rem(c - j + 9, 8), lax.rem(c + j - 1, 8)
         for way, block, to, cond in (
             (0, low, up, (c < 7) & (c >= j - 1)),
             (1, high, dn, (c > 0) & (c + j <= 8)),
         ):
-            src = tok.at[rows] if j == 1 else xbuf.at[block, rows]
-            chain[j, h, way] = start(src, xbuf.at[block, rows], (s, to), cond)
+            chain[j, key, way] = start(ref(block), ref(block), (s, to), cond)
+
+    def arrive(j, key):
+        pl.when(c >= j)(lambda: chain[j, key, 0].wait_recv())
+        pl.when(c + j <= 7)(lambda: chain[j, key, 1].wait_recv())
+
+    def tok_send(j, h):
+        pass_along(j, h, lambda block: xbuf.at[block, pl.ds(2 * h, 2)])
+
+    def last_send(j):
+        pass_along(j, "last", lambda block: last.at[block])
 
     def tok_step(j, h):
-        pl.when(c >= j)(lambda: chain[j, h, 0].wait_recv())
-        pl.when(c + j <= 7)(lambda: chain[j, h, 1].wait_recv())
+        arrive(j, h)
         if j < 7:
             tok_send(j + 1, h)
+
+    def last_step(j):
+        arrive(j, "last")
+        if j < 7:
+            last_send(j + 1)
 
     def one(which, d, zz, rows):
         px, py = (xs(d), y) if which == "x" else (x, ys(d))
@@ -106,68 +119,92 @@
 
     class Gather:
         def __init__(self, zz, own):
-            self.zz = zz
-            self.sib = []
-            self.near = {}
+            self.zz, self.own = zz, own
+            self.sib, self.near, self.far, self.turned, self.passed = [], {}, [], {}, []
             for first, _, r in ORDER:
                 rows = pl.ds(r, 32)
                 src = w.at[rows] if own else one(first, 0, zz, rows)
                 for d in (1, -1):
                     self.near[first, d] = start(src, one(first, 0, zz, rows), to(first, d))
-
-        def pass_on(self):
-            self.far = []
-            for first, _, r in ORDER:
+            for first, second, r in ORDER:
+                self.turn(first, second, r, 0)
+
+        def turn(self, first, second, r, p):
+            ref = one(first, p, self.zz, pl.ds(r, 32))
+            src = w.at[pl.ds(r, 32)] if self.own and p == 0 else ref
+            for d in (1, -1):
+                self.turned[second, p, d] = start(src, ref, to(second, d))
+
+        def half(self, r, d):
+            return pl.ds(r + (0 if d == 1 else 16), 16)
+
+        def pass_turned(self, first, second, r, p):
+            for d in (1, -1):
+                self.turned[second, p, d].wait_recv()
+                px, py = (xs(p), ys(-d)) if second == "y" else (xs(-d), ys(p))
+                ref = wbuf.at[px, py, self.zz, k, self.half(r, d)]
+                self.passed.append(start(ref, ref, to(second, d)))
+
+        def to_sibling(self, second, d, r):
+            ref = line(second, d, self.zz, pl.ds(r, 32))
+            self.sib.append(start(ref, ref, sibling))
+
+        def step1(self):
+            for first, second, r in ORDER:
                 for d in (1, -1):
-                    rows = pl.ds(r + (0 if d == 1 else 16), 16)
                     self.near[first, d].wait_recv()
-                    self.far.append(start(one(first, -d, self.zz, rows), one(first, -d, self.zz, rows), to(first, d)))
-
-        def turn(self):
+                    ref = one(first, -d, self.zz, self.half(r, d))
+                    self.far.append(start(ref, ref, to(first, d)))
+                    self.turn(first, second, r, -d)
+            for first, second, r in ORDER:
+                self.pass_turned(first, second, r, 0)
+
+        def step2(self):
             for copy in self.far:
                 copy.wait_recv()
-            self.near2 = {}
-            for _, second, r in ORDER:
-                ref = line(second, 0, self.zz, pl.ds(r, 32))
-                for d in (1, -1):
-                    self.near2[second, d] = start(ref, ref, to(second, d))
-            for _, second, r in ORDER:
-                ref = line(second, 0, self.zz, pl.ds(r, 32))
-                self.sib.append(start(ref, ref, sibling))
-
-        def pass_on2(self):
-            self.far2 = []
+            for first, second, r in ORDER:
+                self.turn(first, second, r, 2)
+            for first, second, r in ORDER:
+                self.to_sibling(second, 0, r)
+            for p in (1, -1):
+                for first, second, r in ORDER:
+                    self.pass_turned(first, second, r, p)
+
+        def step3(self):
+            for first, second, r in ORDER:
+                self.pass_turned(first, second, r, 2)
             for _, second, r in ORDER:
                 for d in (1, -1):
-                    rows = pl.ds(r + (0 if d == 1 else 16), 16)
-                    self.near2[second, d].wait_recv()
-                    ref = line(second, -d, self.zz, rows)
-                    self.far2.append(start(ref, ref, to(second, d)))
-            for _, second, r in ORDER:
-                for d in (1, -1):
-                    ref = line(second, d, self.zz, pl.ds(r, 32))
-                    self.sib.append(start(ref, ref, sibling))
-
-        def finish(self):
-            for copy in self.far2:
+                    self.to_sibling(second, d, r)
+
+        def step4(self):
+            for copy in self.passed:
                 copy.wait_recv()
             for _, second, r in ORDER:
-                ref = line(second, 2, self.zz, pl.ds(r, 32))
-                self.sib.append(start(ref, ref, sibling))
+                self.to_sibling(second, 2, r)
 
         def wait_sibling(self):
             for copy in self.sib:
                 copy.wait_recv()
 
-    leg_a = start(w.at[pl.ds(0, 32)], legs.at[0], z_up)
-    leg_b = start(w.at[pl.ds(32, 32)], legs.at[1], z_dn)
-    tok_send(1, 0)
-    tok_send(1, 1)
+    def leg(way, r):
+        return start(w.at[pl.ds(32 * way + r, 16)], legs.at[way, pl.ds(r, 16)], z_dn if way else z_up)
+
+    def next_leg(way, r):
+        zz = lax.rem(zh + over, 2)
+        dst = wbuf.at[x, y, zz if way else 1 - zz, k, pl.ds(32 * way + r, 16)]
+        return start(legs.at[way, pl.ds(r, 16)], dst, z_dn if way else z_up)
+
+    leg1 = [leg(way, r) for r in (0, 16) for way in (0, 1)]
     mine = Gather(zh, True)
     keep_w = pltpu.make_async_copy(w, wbuf.at[x, y, zh, k], loc.at[0])
-    keep_x = pltpu.make_async_copy(tok, xbuf.at[c], loc.at[1])
     keep_w.start()
-    keep_x.start()
+    packed[...] = jnp.zeros_like(packed)
+    for j in range(4):
+        xbuf[c, j] = tok[:, j * 128 : (j + 1) * 128]
+        packed[2 * j : 2 * j + 2, :] = tok[ROWS - 16 :, j * 128 : (j + 1) * 128].astype(F32)[14:, :]
+    last_out[...] = packed[...].astype(BF16)
+    handed = start(last_out, last_in, after)
 
     def tables():
         acc[...] = jnp.zeros_like(acc)
@@ -178,74 +215,99 @@
         powers[2] = jnp.exp(rate * (4.0 * ROWS))
         powers[3] = jnp.exp(rate * (16.0 * ROWS))
         powers[4] = jnp.exp(rate * ((4.0 * ROWS) * y.astype(F32)))
-        powers[5] = jnp.exp(rate * (STEPS - 1.0))
-        powers[6] = jnp.exp(rate * (STEPS - 2.0))
         sub = lax.broadcasted_iota(jnp.int32, (SUBS, CH), 0).astype(F32)
         for n in range(MODES):
             r = poles[n : n + 1, :] * (-STEPS / SEQ)
             head_w[n] = jnp.exp(r * sub)
             tail_w[n] = jnp.exp(r * (SUBS - 1.0 - sub))
 
+    def add_dot(cc, left, right):
+        for g in range(3):
+            dot = jnp.dot(left, right(pl.ds(g * CH, CH)), preferred_element_type=F32)
+            for lg in range(4):
+                acc[4 * g + lg] += dot[:, lg * 128 : (lg + 1) * 128]
+
+    row = lax.broadcasted_iota(jnp.int32, (TOP, 128), 0)
+
+    def features(cc, j):
+        top = jnp.where((row >= 2 * j) & (row < 2 * j + 2), last[cc].astype(F32), 0.0).astype(BF16)
+        return jnp.concatenate([top, xbuf[cc, j]], axis=0)
+
+    def dot_z(zz, cc):
+        px, py = lax.div(cc, 2), lax.rem(cc, 2) * 2
+        left = jnp.concatenate([features(cc, zz), features(cc, zz + 2)], axis=1)
+        add_dot(cc, left, lambda cols: wbuf[px, pl.ds(py, 2), zz, :, :, cols].reshape(256, CH))
+
+    def dot_y(p, cc):
+        px, py = lax.div(cc, 2), lax.rem(cc, 2) * 2 + p
+        left = jnp.concatenate([features(cc, 2 * p), features(cc, 2 * p + 1)], axis=1)
+        add_dot(cc, left, lambda cols: wbuf[px, py, :, :, :, cols].reshape(256, CH))
+
+    def dots(kind, which, lo, hi):
+        def body(j, _):
+            pl.when(c >= j)(lambda: kind(which, lax.rem(c - j + 8, 8)))
+            pl.when((j > 0) & (c + j <= 7))(lambda: kind(which, lax.rem(c + j, 8)))
+            return 0
+
+        lax.fori_loop(lo, hi, body, 0)
+
+    mine.step1()
+    leg2 = []
+    for copy, (r, way) in zip(leg1, ((0, 0), (0, 1), (16, 0), (16, 1))):
+        copy.wait_recv()
+        leg2.append(next_leg(way, r))
+    tok_send(1, 0)
+    tok_send(1, 1)
+    keep_w.wait()
+    mine.step2()
+    tables()
+    mine.step3()
+    handed.wait_recv()
+    last[c] = jnp.where(s > 0, last_in[...].astype(F32), 0.0).astype(BF16)
+    last_send(1)
     tok_step(1, 0)
-    mine.pass_on()
+    for copy in leg2:
+        copy.wait_recv()
+    theirs = Gather(1 - zh, False)
     tok_step(1, 1)
-    keep_w.wait()
-    mine.turn()
-    tables()
+    last_step(1)
+    mine.step4()
     tok_step(2, 0)
-    leg_a.wait_recv()
-    leg_c = start(legs.at[0], wbuf.at[x, y, 1 - z_up_zh(zh, over), k, pl.ds(0, 32)], z_up)
-    leg_b.wait_recv()
-    leg_d = start(legs.at[1], wbuf.at[x, y, z_up_zh(zh, over), k, pl.ds(32, 32)], z_dn)
+    theirs.step1()
     tok_step(2, 1)
-    mine.pass_on2()
+    last_step(2)
+    mine.wait_sibling()
+    dots(dot_z, zh, 0, 2)
+    theirs.step2()
     tok_step(3, 0)
     tok_step(3, 1)
-    mine.finish()
-    leg_c.wait_recv()
-    leg_d.wait_recv()
-    theirs = Gather(1 - zh, False)
+    last_step(3)
+    theirs.step3()
+    dots(dot_z, zh, 2, 4)
     tok_step(4, 0)
-    theirs.pass_on()
     tok_step(4, 1)
-    theirs.turn()
+    last_step(4)
+    theirs.step4()
     tok_step(5, 0)
     tok_step(5, 1)
-    theirs.pass_on2()
+    last_step(5)
+    dots(dot_z, zh, 4, 6)
+    theirs.wait_sibling()
+    dots(dot_z, 1 - zh, 0, 6)
     tok_step(6, 0)
-    mine.wait_sibling()
     tok_step(6, 1)
-    theirs.finish()
-    keep_x.wait()
-    theirs.wait_sibling()
-
-    def dot_chunk(cc):
-        px, py = lax.div(cc, 2), lax.rem(cc, 2) * 2
-        for g in range(3):
-            cols = pl.ds(g * CH, CH)
-            part = wbuf[px, pl.ds(py, 2), :, :, :, cols].reshape(CH, CH)
-            dot = jnp.dot(xbuf[cc], part, preferred_element_type=F32)
-            for lg in range(4):
-                acc[4 * g + lg, 8:, :] += dot[:, lg * 128 : (lg + 1) * 128]
-
-    def dots(lo, hi):
-        def body(j, _):
-            pl.when(c >= j)(lambda: dot_chunk(lax.rem(c - j + 8, 8)))
-            pl.when((j > 0) & (c + j <= 7))(lambda: dot_chunk(lax.rem(c + j, 8)))
-            return 0
-
-        lax.fori_loop(lo, hi, body, 0)
-
-    dots(0, 7)
+    last_step(6)
+    dots(dot_z, zh, 6, 7)
+    dots(dot_z, 1 - zh, 6, 7)
     tok_step(7, 0)
+    last_step(7)
+    dots(dot_y, 0, 7, 8)
     tok_step(7, 1)
-    dots(7, 8)
-
-    for r in range(2):
-        for i in range(12):
-            row, cols = 3 * r + i // 4, (i % 4) * 128
-            halo_out[row : row + 1, cols : cols + 128] = rounded(acc[i, 6 + ROWS + r : 7 + ROWS + r, :])
-    halo = start(halo_out, halo_in, after, s < 63)
+    dots(dot_y, 1, 7, 8)
+    for i in range(12):
+        for r in range(2):
+            two = [acc[i, 2 * j + r : 2 * j + r + 1, :] for j in range(4)]
+            acc[i, TOP - 2 + r : TOP - 1 + r, :] = total(two)
 
     def lanes(lg):
         return pl.ds(lg * 128, 128)
@@ -270,39 +332,19 @@
 
         def body(i, held):
             k1, k2, v1, v2, st = held
-            k0, v0 = lk(8 + i), lv(8 + i)
+            k0, v0 = lk(TOP + i), lv(TOP + i)
             g = gate(fk, fv, (k0, k1, k2), (v0, v1, v2))
             gbuf[i, :, lanes(lg)] = g
             return k0, k1, v0, v1, tuple(a[n] * st[n] + g for n in range(MODES))
 
         zero = tuple(jnp.zeros((SUBS, 128), F32) for _ in range(MODES))
-        held = lax.fori_loop(0, STEPS, body, (lk(7), lk(6), lv(7), lv(6), zero), unroll=4)
+        held = lax.fori_loop(0, STEPS, body, (lk(TOP - 1), lk(TOP - 2), lv(TOP - 1), lv(TOP - 2), zero), unroll=4)
         for n in range(MODES):
             ends[n, :, lanes(lg)] = held[4][n]
+            state[n : n + 1, lanes(lg)] = jnp.sum(tail_w[n, :, lanes(lg)] * held[4][n], axis=0, keepdims=True)
 
     for lg in range(4):
         pass_a(lg)
-
-    @pl.when(s > 0)
-    def _():
-        halo.wait_recv()
-        for r in range(2):
-            for i in range(12):
-                row, cols = 3 * r + i // 4, (i % 4) * 128
-                acc[i, 6 + r : 7 + r, :] = halo_in[row : row + 1, cols : cols + 128]
-
-    for lg in range(4):
-        (fk, lk), (fv, lv) = filter_of(1, lg), filter_of(2, lg)
-        pk, pv = [lk(6 + i) for i in range(4)], [lv(6 + i) for i in range(4)]
-        g0 = gate(fk, fv, pk[2::-1], pv[2::-1])
-        g1 = gate(fk, fv, pk[3:0:-1], pv[3:0:-1])
-        d0, d1 = g0 - gbuf[0, :, lanes(lg)], g1 - gbuf[1, :, lanes(lg)]
-        gbuf[0, :, lanes(lg)] = g0
-        gbuf[1, :, lanes(lg)] = g1
-        for n in range(MODES):
-            end = ends[n, :, lanes(lg)] + powers[5, n : n + 1, lanes(lg)] * d0 + powers[6, n : n + 1, lanes(lg)] * d1
-            ends[n, :, lanes(lg)] = end
-            state[n : n + 1, lanes(lg)] = jnp.sum(tail_w[n, :, lanes(lg)] * end, axis=0, keepdims=True)
 
     def pass_b(lg):
         fq, lq = filter_of(0, lg)
@@ -311,7 +353,7 @@
 
         def body(i, held):
             q1, q2, st = held
-            q0 = lq(8 + i)
+            q0 = lq(TOP + i)
             qbuf[i, :, lanes(lg)] = fq(q0, q1, q2)
             g = gbuf[i, :, lanes(lg)]
             st = tuple(a[n] * st[n] + g for n in range(MODES))
@@ -319,7 +361,7 @@
             return q0, q1, st
 
         zero = tuple(jnp.zeros((SUBS, 128), F32) for _ in range(MODES))
-        lax.fori_loop(0, STEPS, body, (lq(7), lq(6), zero), unroll=2)
+        lax.fori_loop(0, STEPS, body, (lq(TOP - 1), lq(TOP - 2), zero), unroll=2)
         sub = lax.broadcasted_iota(jnp.int32, (SUBS, 128), 0)
 
         def down(value, by):
@@ -398,10 +440,6 @@
             pl.when(cond)(lambda copy=copy: copy.wait_send())
 
 
-def z_up_zh(zh, over):
-    return lax.rem(zh + over, 2)
-
-
 def total(values):
     while len(values) > 1:
         values = [a + b for a, b in zip(values[::2], values[1::2])] + values[len(values) & ~1 :]
@@ -414,7 +452,7 @@
     table = pltpu.VMEM((MODES, SUBS, CH), F32)
     full, part = pltpu.VMEM((MODES, CH), F32), pltpu.VMEM((MODES, CH // 2), F32)
     parts4 = pltpu.VMEM((4, MODES, CH // 2), F32)
-    halo = pltpu.VMEM((8, CH), F32)
+    last = pltpu.VMEM((16, 128), BF16)
     return pl.pallas_call(
         kernel,
         out_shape=jax.ShapeDtypeStruct((ROWS, CH), BF16),
@@ -422,17 +460,18 @@
         out_specs=vmem,
         scratch_shapes=[
             pltpu.VMEM((4, 4, 2, 2, DEPTH, 3 * CH), BF16),
-            pltpu.VMEM((8, ROWS, CH), BF16),
-            pltpu.VMEM((12, 8 + ROWS, 128), F32),
+            pltpu.VMEM((8, 4, ROWS, 128), BF16),
+            pltpu.VMEM((12, TOP + ROWS, 128), F32),
             pltpu.VMEM((2, DEPTH // 2, 3 * CH), BF16),
             block, block, block,
             pltpu.VMEM((4, ROWS, 128), F32),
             table, table, full, table, table,
-            pltpu.VMEM((7, MODES, CH), F32),
-            full, full, part, parts4, part, parts4, part, part, part, part, full, halo, halo,
+            pltpu.VMEM((5, MODES, CH), F32),
+            full, full, part, parts4, part, parts4, part, part, part, part, full,
+            pltpu.VMEM((16, 128), F32), last, last, pltpu.VMEM((8, 16, 128), BF16),
             pltpu.SemaphoreType.DMA((COPIES,)),
             pltpu.SemaphoreType.DMA((COPIES,)),
-            pltpu.SemaphoreType.DMA((2,)),
+            pltpu.SemaphoreType.DMA((1,)),
         ],
         compiler_params=pltpu.CompilerParams(
             collective_id=0, has_side_effects=True, vmem_limit_bytes=40 * 1024 * 1024

time: 112 us -> 103 us (0.920)
  Pallas kernels: 110 us -> 101 us
    pallas_call x1, Pallas kernels: 110 us -> 101 us  [local(): pl.pallas_call(kernel, out_shape=jax.ShapeDtypeStruct((ROWS, CH), BF16),...]
where the time goes in v2:
time: 103 us
  Pallas kernels  101 us (98%)
  local copies, waits for them, and re-layouts  1.73 us (2%)
    pallas_call x1, Pallas kernels, local(): pl.pallas_call(kernel, out_shape=jax.ShapeDtypeStruct((ROWS, CH), BF16),...  101 us

profile of v2, /device:TPU:1, one launch (start us, length us, event | category | flops | bytes accessed | tf_op | source)
XLA Modules:
  0.0 103.1 jit_solution(14589427091611866612)
XLA Ops:
  0.0 0.0 copy-start
  0.0 0.0 copy-start.1
  0.0 0.0 copy-start.2
  0.0 0.0 copy-start.3
  0.0 0.0 copy-start.4
  0.0 1.0 copy.9
  1.0 0.0 copy-done
  1.0 0.0 copy-done.1
  1.0 0.0 copy-done.2
  1.1 0.0 copy-done.3
  1.1 0.0 copy-done.4
  1.1 101.4 %shard_map.64 = bf16[256,512]{1,0:T(8,128)(2,1)S(1)} custom-call(bf16[256,512]{1,0:T(8,128)(2,1)S(1)} %copy-done, bf16[64,1536]{1,0:T(8,128)(2,1)S(1)} %bitcast.3, f32[3,3,512]{2,1,0:T(4,128)S(1)} %copy-done.3, f32[16,512]{1,0:T(8,128)S(1)} %copy-done.1, f32[16,512]{1,0:T(8,128)S(1)} %copy-done.2, f32[1,512]{1,0:T(1,128)S(1)} %bitcast.4), custom_call_target="tpu_custom_call" | custom-call | tf_op jit(solution)/shard_map/pallas_call | solution.py:456
  102.4 0.7 copy.11
Async XLA Ops:
  0.0 1.0 %copy-start = (bf16[256,512]{1,0:T(8,128)(2,1)S(1)}, bf16[256,512]{1,0:T(8,128)(2,1)}, u32[]{:S(2)}) copy-start(bf16[256,512]{1,0:T(8,128)(2,1)} %tok.1) | copy-start | bytes 786436
  0.0 1.0 %copy-start.1 = (f32[16,512]{1,0:T(8,128)S(1)}, f32[16,512]{1,0:T(8,128)}, u32[]{:S(2)}) copy-start(f32[16,512]{1,0:T(8,128)} %res.1) | copy-start | bytes 98308
  0.0 1.0 %copy-start.2 = (f32[16,512]{1,0:T(8,128)S(1)}, f32[16,512]{1,0:T(8,128)}, u32[]{:S(2)}) copy-start(f32[16,512]{1,0:T(8,128)} %poles.1) | copy-start | bytes 98308
  0.0 1.0 %copy-start.3 = (f32[3,3,512]{2,1,0:T(4,128)S(1)}, f32[3,3,512]{2,1,0:T(4,128)}, u32[]{:S(2)}) copy-start(f32[3,3,512]{2,1,0:T(4,128)} %taps.1) | copy-start | bytes 55300
  0.0 1.0 %copy-start.4 = (f32[512]{0:T(512)S(1)}, f32[512]{0:T(512)}, u32[]{:S(2)}) copy-start(f32[512]{0:T(512)} %param.11) | copy-start | bytes 6148

commit v3 on v2

--- a/solution.py
+++ b/solution.py
@@ -25,7 +25,7 @@
 def kernel(
     tok, w, taps, res, poles, skip, out,
     wbuf, xbuf, acc, legs, gbuf, ybuf, qbuf, obuf, ends, prefix, decay, tail_w, head_w, powers,
-    state, sib_state, c_msg, y_in, r_msg, x_in, z_msg, z_in, k_msg, k_in, carry, packed, last_out, last_in, last,
+    state, sib_state, c_msg, y_in, z_msg, z_in, k_msg, k_in, carry, packed, last_out, last_in, last,
     send, recv, loc,
 ):
     s, c = lax.axis_index("seq"), lax.axis_index("chan")
@@ -52,13 +52,13 @@
 
     barrier = pltpu.get_barrier_semaphore()
     partners = [sibling, opposite, z_up, z_dn, (s, up), (s, dn), after, before]
-    for d in (1, 2, 3):
-        partners += [at(px=xs(d)), at(py=ys(d))]
+    steps = [(dx, dy) for dx in range(4) for dy in range(4) if dx or dy]
+    partners += [at(px=xs(dx), py=ys(dy)) for dx, dy in steps]
     for partner in partners:
         pl.semaphore_signal(barrier, inc=1, device_id=partner, device_id_type=MESH)
     pl.semaphore_wait(barrier, len(partners))
 
-    sent = []
+    sent, done = [], []
 
     def start(src, dst, to, cond=None):
         i = len(sent)
@@ -73,6 +73,14 @@
         sent.append((copy, cond))
         return copy
 
+    def drain():
+        for copy, cond in sent[len(done) :]:
+            if cond is None:
+                copy.wait_send()
+            else:
+                pl.when(cond)(lambda copy=copy: copy.wait_send())
+            done.append(copy)
+
     chain = {}
 
     def pass_along(j, key, ref):
@@ -213,8 +221,6 @@
         powers[0] = jnp.exp(rate * ROWS)
         powers[1] = jnp.exp(rate * (2.0 * ROWS))
         powers[2] = jnp.exp(rate * (4.0 * ROWS))
-        powers[3] = jnp.exp(rate * (16.0 * ROWS))
-        powers[4] = jnp.exp(rate * ((4.0 * ROWS) * y.astype(F32)))
         sub = lax.broadcasted_iota(jnp.int32, (SUBS, CH), 0).astype(F32)
         for n in range(MODES):
             r = poles[n : n + 1, :] * (-STEPS / SEQ)
@@ -269,25 +275,25 @@
     for copy in leg2:
         copy.wait_recv()
     theirs = Gather(1 - zh, False)
+    mine.step4()
     tok_step(1, 1)
     last_step(1)
-    mine.step4()
+    theirs.step1()
     tok_step(2, 0)
-    theirs.step1()
+    last_step(2)
     tok_step(2, 1)
-    last_step(2)
+    theirs.step2()
+    tok_step(3, 0)
     mine.wait_sibling()
     dots(dot_z, zh, 0, 2)
-    theirs.step2()
-    tok_step(3, 0)
     tok_step(3, 1)
     last_step(3)
     theirs.step3()
+    tok_step(4, 0)
     dots(dot_z, zh, 2, 4)
-    tok_step(4, 0)
     tok_step(4, 1)
+    theirs.step4()
     last_step(4)
-    theirs.step4()
     tok_step(5, 0)
     tok_step(5, 1)
     last_step(5)
@@ -310,7 +316,7 @@
             acc[i, TOP - 2 + r : TOP - 1 + r, :] = total(two)
 
     def lanes(lg):
-        return pl.ds(lg * 128, 128)
+        return pl.ds(pl.multiple_of(lg * 128, 128), 128)
 
     def rows_of(ref, lg):
         return [jnp.broadcast_to(ref[n : n + 1, lanes(lg)], (SUBS, 128)) for n in range(MODES)]
@@ -343,8 +349,15 @@
             ends[n, :, lanes(lg)] = held[4][n]
             state[n : n + 1, lanes(lg)] = jnp.sum(tail_w[n, :, lanes(lg)] * held[4][n], axis=0, keepdims=True)
 
-    for lg in range(4):
+    half = pl.ds(pl.multiple_of(k * 256, 256), 256)
+    other = pl.ds(pl.multiple_of((1 - k) * 256, 256), 256)
+    own_groups, other_groups = (2 * k, 2 * k + 1), (2 - 2 * k, 3 - 2 * k)
+    for lg in other_groups:
         pass_a(lg)
+    first = start(state.at[:, other], sib_state.at[:, other], sibling)
+    for lg in own_groups:
+        pass_a(lg)
+    second = start(state.at[:, half], sib_state.at[:, half], sibling)
 
     def pass_b(lg):
         fq, lq = filter_of(0, lg)
@@ -373,46 +386,36 @@
                 v = v + head_w[n, by : by + 1, lanes(lg)] * down(v, by)
             prefix[n, :, lanes(lg)] = v
 
-    half = pl.ds(pl.multiple_of(k * 256, 256), 256)
-    other = pl.ds(pl.multiple_of((1 - k) * 256, 256), 256)
-    first = start(state, sib_state, sibling)
-    pass_b(0)
     first.wait_recv()
     own, sib = state[:, half], sib_state[:, half]
     chip = powers[0, :, half] * jnp.where(k == 0, own, sib) + jnp.where(k == 0, sib, own)
     c_msg[...] = chip
-    y_in[y] = chip
-    level = [start(c_msg, y_in.at[y], at(py=ys(d))) for d in (1, 2, 3)]
+    q = 4 * x + y
+    level = []
+    for dx, dy in steps:
+        later = 4 * xs(dx) + ys(dy) > q
+        level.append(start(c_msg, y_in.at[q], at(px=xs(dx), py=ys(dy)), later))
+    pass_b(0)
     pass_b(1)
-    for copy in level:
-        copy.wait_recv()
+    drain()
+    for (dx, dy), copy in zip(steps, level):
+        pl.when(4 * xs(-dx) + ys(-dy) < q)(lambda copy=copy: copy.wait_recv())
     d4 = powers[2, :, half]
-    row, early = jnp.zeros_like(chip), jnp.zeros_like(chip)
-    for i in range(4):
-        got = y_in[i]
-        row = row * d4 + got
-        early = jnp.where(i < y, early * d4 + got, early)
-    r_msg[...] = row
-    x_in[x] = row
-    level = [start(r_msg, x_in.at[x], at(px=xs(d))) for d in (1, 2, 3)]
-    pass_b(2)
-    for copy in level:
-        copy.wait_recv()
-    d16, lead = powers[3, :, half], jnp.zeros_like(chip)
-    for i in range(4):
-        lead = jnp.where(i < x, lead * d16 + x_in[i], lead)
-    plane = early + powers[4, :, half] * lead
+    plane = lax.fori_loop(0, q, lambda i, got: got * d4 + y_in[i], jnp.zeros_like(chip))
     z_msg[...] = jnp.where(zh == 0, d4 * plane + chip, plane)
     level = start(z_msg, z_in, opposite)
+    second.wait_recv()
+    pass_b(2)
     pass_b(3)
     level.wait_recv()
     into = powers[1, :, half] * plane + z_in[...]
     k_msg[...] = into
     level = start(k_msg, k_in, sibling)
-    carry[:, half] = into
-    level.wait_recv()
-    carry[:, other] = k_in[...]
-    carry[...] = jnp.where(k == 0, carry[...], powers[0] * carry[...] + sib_state[...])
+
+    def keep(where, value):
+        carry[:, where] = jnp.where(k == 0, value, powers[0, :, where] * value + sib_state[:, where])
+
+    keep(half, into)
 
     def pass_c(lg):
         a, r = rows_of(decay, lg), rows_of(res, lg)
@@ -430,14 +433,14 @@
         lax.fori_loop(0, STEPS, body, ws, unroll=4)
         out[:, lanes(lg)] = obuf[lg].astype(BF16)
 
-    for lg in range(4):
+    for lg in own_groups:
         pass_c(lg)
-
-    for copy, cond in sent:
-        if cond is None:
-            copy.wait_send()
-        else:
-            pl.when(cond)(lambda copy=copy: copy.wait_send())
+    level.wait_recv()
+    keep(other, k_in[...])
+    for lg in other_groups:
+        pass_c(lg)
+
+    drain()
 
 
 def total(values):
@@ -451,7 +454,6 @@
     block = pltpu.VMEM((STEPS, SUBS, CH), F32)
     table = pltpu.VMEM((MODES, SUBS, CH), F32)
     full, part = pltpu.VMEM((MODES, CH), F32), pltpu.VMEM((MODES, CH // 2), F32)
-    parts4 = pltpu.VMEM((4, MODES, CH // 2), F32)
     last = pltpu.VMEM((16, 128), BF16)
     return pl.pallas_call(
         kernel,
@@ -466,8 +468,8 @@
             block, block, block,
             pltpu.VMEM((4, ROWS, 128), F32),
             table, table, full, table, table,
-            pltpu.VMEM((5, MODES, CH), F32),
-            full, full, part, parts4, part, parts4, part, part, part, part, full,
+            pltpu.VMEM((3, MODES, CH), F32),
+            full, full, part, pltpu.VMEM((16, MODES, CH // 2), F32), part, part, part, part, full,
             pltpu.VMEM((16, 128), F32), last, last, pltpu.VMEM((8, 16, 128), BF16),
             pltpu.SemaphoreType.DMA((COPIES,)),
             pltpu.SemaphoreType.DMA((COPIES,)),

time: 103 us -> 98.6 us (0.957)
  the two profiles are of different devices: /device:TPU:1 before, /device:TPU:5 now
where the time goes in v3:
time: 98.6 us; the launch traced here: 98.5 us
  Pallas kernels  96.7 us (98%)
  local copies, waits for them, and re-layouts  1.73 us (2%)
    pallas_call x1, Pallas kernels, local(): pl.pallas_call(kernel, out_shape=jax.ShapeDtypeStruct((ROWS, CH), BF16),...  96.7 us

profile of v3, /device:TPU:5, one launch (start us, length us, event | category | flops | bytes accessed | tf_op | source)
XLA Modules:
  0.0 98.5 jit_solution(80222911816370144)
XLA Ops:
  0.0 0.0 copy-start
  0.0 0.0 copy-start.1
  0.0 0.0 copy-start.2
  0.0 0.0 copy-start.3
  0.0 0.0 copy-start.4
  0.0 1.0 copy.9
  1.0 0.0 copy-done
  1.0 0.0 copy-done.1
  1.0 0.0 copy-done.2
  1.1 0.0 copy-done.3
  1.1 0.0 copy-done.4
  1.1 96.7 %shard_map.64 = bf16[256,512]{1,0:T(8,128)(2,1)S(1)} custom-call(bf16[256,512]{1,0:T(8,128)(2,1)S(1)} %copy-done, bf16[64,1536]{1,0:T(8,128)(2,1)S(1)} %bitcast.3, f32[3,3,512]{2,1,0:T(4,128)S(1)} %copy-done.3, f32[16,512]{1,0:T(8,128)S(1)} %copy-done.1, f32[16,512]{1,0:T(8,128)S(1)} %copy-done.2, f32[1,512]{1,0:T(1,128)S(1)} %bitcast.4), custom_call_target="tpu_custom_call" | custom-call | tf_op jit(solution)/shard_map/pallas_call | solution.py:458
  97.8 0.7 copy.11
Async XLA Ops:
  0.0 1.0 %copy-start = (bf16[256,512]{1,0:T(8,128)(2,1)S(1)}, bf16[256,512]{1,0:T(8,128)(2,1)}, u32[]{:S(2)}) copy-start(bf16[256,512]{1,0:T(8,128)(2,1)} %tok.1) | copy-start | bytes 786436
  0.0 1.0 %copy-start.1 = (f32[16,512]{1,0:T(8,128)S(1)}, f32[16,512]{1,0:T(8,128)}, u32[]{:S(2)}) copy-start(f32[16,512]{1,0:T(8,128)} %res.1) | copy-start | bytes 98308
  0.0 1.0 %copy-start.2 = (f32[16,512]{1,0:T(8,128)S(1)}, f32[16,512]{1,0:T(8,128)}, u32[]{:S(2)}) copy-start(f32[16,512]{1,0:T(8,128)} %poles.1) | copy-start | bytes 98308
  0.0 1.0 %copy-start.3 = (f32[3,3,512]{2,1,0:T(4,128)S(1)}, f32[3,3,512]{2,1,0:T(4,128)}, u32[]{:S(2)}) copy-start(f32[3,3,512]{2,1,0:T(4,128)} %taps.1) | copy-start | bytes 55300
  0.0 1.0 %copy-start.4 = (f32[512]{0:T(512)S(1)}, f32[512]{0:T(512)}, u32[]{:S(2)}) copy-start(f32[512]{0:T(512)} %param.11) | copy-start | bytes 6148

commit v4 on v3

--- a/solution.py
+++ b/solution.py
@@ -15,7 +15,7 @@
 SUBS = 8
 STEPS = ROWS // SUBS
 TOP = 16
-COPIES = 176
+SENDS, RECVS = 68, 81
 
 
 def rounded(value):
@@ -58,20 +58,32 @@
         pl.semaphore_signal(barrier, inc=1, device_id=partner, device_id_type=MESH)
     pl.semaphore_wait(barrier, len(partners))
 
-    sent, done = [], []
-
-    def start(src, dst, to, cond=None):
-        i = len(sent)
+    sent, done, send_ids, recv_ids = [], [], {}, {}
+
+    def start(src, dst, to, cond=None, out_group=None, in_group=None):
+        out_id = send_ids.setdefault(out_group or ("one", len(send_ids)), len(send_ids))
+        in_id = recv_ids.setdefault(in_group or ("one", len(recv_ids)), len(recv_ids))
         copy = pltpu.make_async_remote_copy(
-            src_ref=src, dst_ref=dst, send_sem=send.at[i], recv_sem=recv.at[i],
+            src_ref=src, dst_ref=dst, send_sem=send.at[out_id], recv_sem=recv.at[in_id],
             device_id=to, device_id_type=MESH,
         )
         if cond is None:
             copy.start()
         else:
             pl.when(cond)(lambda: copy.start())
-        sent.append((copy, cond))
+        if out_group is None:
+            sent.append((copy, cond))
         return copy
+
+    def of_group(blocks, out_group=None, in_group=None):
+        ref = {
+            1: wbuf.at[0, 0, 0, 0], 2: wbuf.at[0, 0, 0], 4: wbuf.at[0, 0],
+            8: wbuf.at[0, pl.ds(0, 4), 0], 16: wbuf.at[0], 32: wbuf.at[pl.ds(0, 2)],
+        }[blocks]
+        return pltpu.make_async_remote_copy(
+            src_ref=ref, dst_ref=ref, send_sem=send.at[send_ids.get(out_group, 0)],
+            recv_sem=recv.at[recv_ids.get(in_group, 0)], device_id=sibling, device_id_type=MESH,
+        )
 
     def drain():
         for copy, cond in sent[len(done) :]:
@@ -81,6 +93,10 @@
                 pl.when(cond)(lambda copy=copy: copy.wait_send())
             done.append(copy)
 
+    def drain_groups():
+        for group, blocks in (("leg", 2), ("near", 4), ("far", 2), ("turned", 16), ("passed", 8), ("sib", 32)):
+            of_group(blocks, out_group=group).wait_send()
+
     chain = {}
 
     def pass_along(j, key, ref):
@@ -126,85 +142,85 @@
     ORDER = (("x", "y", 0), ("y", "x", 32))
 
     class Gather:
-        def __init__(self, zz, own):
-            self.zz, self.own = zz, own
-            self.sib, self.near, self.far, self.turned, self.passed = [], {}, [], {}, []
+        def __init__(self, zz, name):
+            self.zz, self.name = zz, name
             for first, _, r in ORDER:
                 rows = pl.ds(r, 32)
-                src = w.at[rows] if own else one(first, 0, zz, rows)
+                src = w.at[rows] if name == "mine" else one(first, 0, zz, rows)
                 for d in (1, -1):
-                    self.near[first, d] = start(src, one(first, 0, zz, rows), to(first, d))
+                    self.put(src, one(first, 0, zz, rows), to(first, d), "near")
             for first, second, r in ORDER:
-                self.turn(first, second, r, 0)
-
-        def turn(self, first, second, r, p):
+                self.turn(first, second, r, 0, "turned0")
+
+        def put(self, src, dst, where, group, in_group=None):
+            start(src, dst, where, out_group=group, in_group=(self.name, in_group or group))
+
+        def got(self, group, blocks):
+            of_group(blocks, in_group=(self.name, group)).wait_recv()
+
+        def turn(self, first, second, r, p, group):
             ref = one(first, p, self.zz, pl.ds(r, 32))
-            src = w.at[pl.ds(r, 32)] if self.own and p == 0 else ref
+            src = w.at[pl.ds(r, 32)] if self.name == "mine" and p == 0 else ref
             for d in (1, -1):
-                self.turned[second, p, d] = start(src, ref, to(second, d))
+                self.put(src, ref, to(second, d), "turned", group)
 
         def half(self, r, d):
             return pl.ds(r + (0 if d == 1 else 16), 16)
 
-        def pass_turned(self, first, second, r, p):
-            for d in (1, -1):
-                self.turned[second, p, d].wait_recv()
-                px, py = (xs(p), ys(-d)) if second == "y" else (xs(-d), ys(p))
-                ref = wbuf.at[px, py, self.zz, k, self.half(r, d)]
-                self.passed.append(start(ref, ref, to(second, d)))
-
-        def to_sibling(self, second, d, r):
-            ref = line(second, d, self.zz, pl.ds(r, 32))
-            self.sib.append(start(ref, ref, sibling))
-
-        def step1(self):
+        def pass_turned(self, p):
             for first, second, r in ORDER:
                 for d in (1, -1):
-                    self.near[first, d].wait_recv()
+                    px, py = (xs(p), ys(-d)) if second == "y" else (xs(-d), ys(p))
+                    ref = wbuf.at[px, py, self.zz, k, self.half(r, d)]
+                    self.put(ref, ref, to(second, d), "passed")
+
+        def to_sibling(self, d):
+            for _, second, r in ORDER:
+                ref = line(second, d, self.zz, pl.ds(r, 32))
+                self.put(ref, ref, sibling, "sib")
+
+        def step1(self):
+            self.got("near", 2)
+            for first, second, r in ORDER:
+                for d in (1, -1):
                     ref = one(first, -d, self.zz, self.half(r, d))
-                    self.far.append(start(ref, ref, to(first, d)))
-                    self.turn(first, second, r, -d)
+                    self.put(ref, ref, to(first, d), "far")
+                    self.turn(first, second, r, -d, "turned1")
+            self.got("turned0", 2)
+            self.pass_turned(0)
+
+        def step2(self):
+            self.got("far", 1)
             for first, second, r in ORDER:
-                self.pass_turned(first, second, r, 0)
-
-        def step2(self):
-            for copy in self.far:
-                copy.wait_recv()
-            for first, second, r in ORDER:
-                self.turn(first, second, r, 2)
-            for first, second, r in ORDER:
-                self.to_sibling(second, 0, r)
-            for p in (1, -1):
-                for first, second, r in ORDER:
-                    self.pass_turned(first, second, r, p)
+                self.turn(first, second, r, 2, "turned2")
+            self.to_sibling(0)
+            self.got("turned1", 4)
+            self.pass_turned(1)
+            self.pass_turned(-1)
 
         def step3(self):
-            for first, second, r in ORDER:
-                self.pass_turned(first, second, r, 2)
-            for _, second, r in ORDER:
-                for d in (1, -1):
-                    self.to_sibling(second, d, r)
+            self.got("turned2", 2)
+            self.pass_turned(2)
+            self.to_sibling(1)
+            self.to_sibling(-1)
 
         def step4(self):
-            for copy in self.passed:
-                copy.wait_recv()
-            for _, second, r in ORDER:
-                self.to_sibling(second, 2, r)
+            self.got("passed", 4)
+            self.to_sibling(2)
 
         def wait_sibling(self):
-            for copy in self.sib:
-                copy.wait_recv()
+            self.got("sib", 16)
 
     def leg(way, r):
-        return start(w.at[pl.ds(32 * way + r, 16)], legs.at[way, pl.ds(r, 16)], z_dn if way else z_up)
+        return start(w.at[pl.ds(32 * way + r, 16)], legs.at[way, pl.ds(r, 16)], z_dn if way else z_up, None, "leg")
 
     def next_leg(way, r):
         zz = lax.rem(zh + over, 2)
         dst = wbuf.at[x, y, zz if way else 1 - zz, k, pl.ds(32 * way + r, 16)]
-        return start(legs.at[way, pl.ds(r, 16)], dst, z_dn if way else z_up)
+        return start(legs.at[way, pl.ds(r, 16)], dst, z_dn if way else z_up, None, "leg", "leg2")
 
     leg1 = [leg(way, r) for r in (0, 16) for way in (0, 1)]
-    mine = Gather(zh, True)
+    mine = Gather(zh, "mine")
     keep_w = pltpu.make_async_copy(w, wbuf.at[x, y, zh, k], loc.at[0])
     keep_w.start()
     packed[...] = jnp.zeros_like(packed)
@@ -258,10 +274,9 @@
         lax.fori_loop(lo, hi, body, 0)
 
     mine.step1()
-    leg2 = []
     for copy, (r, way) in zip(leg1, ((0, 0), (0, 1), (16, 0), (16, 1))):
         copy.wait_recv()
-        leg2.append(next_leg(way, r))
+        next_leg(way, r)
     tok_send(1, 0)
     tok_send(1, 1)
     keep_w.wait()
@@ -272,9 +287,8 @@
     last[c] = jnp.where(s > 0, last_in[...].astype(F32), 0.0).astype(BF16)
     last_send(1)
     tok_step(1, 0)
-    for copy in leg2:
-        copy.wait_recv()
-    theirs = Gather(1 - zh, False)
+    of_group(1, in_group="leg2").wait_recv()
+    theirs = Gather(1 - zh, "theirs")
     mine.step4()
     tok_step(1, 1)
     last_step(1)
@@ -398,6 +412,7 @@
     pass_b(0)
     pass_b(1)
     drain()
+    drain_groups()
     for (dx, dy), copy in zip(steps, level):
         pl.when(4 * xs(-dx) + ys(-dy) < q)(lambda copy=copy: copy.wait_recv())
     d4 = powers[2, :, half]
@@ -471,8 +486,8 @@
             pltpu.VMEM((3, MODES, CH), F32),
             full, full, part, pltpu.VMEM((16, MODES, CH // 2), F32), part, part, part, part, full,
             pltpu.VMEM((16, 128), F32), last, last, pltpu.VMEM((8, 16, 128), BF16),
-            pltpu.SemaphoreType.DMA((COPIES,)),
-            pltpu.SemaphoreType.DMA((COPIES,)),
+            pltpu.SemaphoreType.DMA((SENDS,)),
+            pltpu.SemaphoreType.DMA((RECVS,)),
             pltpu.SemaphoreType.DMA((1,)),
         ],
         compiler_params=pltpu.CompilerParams(

time: 98.6 us -> 96 us (0.974)
  Pallas kernels: 96.7 us -> 94.1 us
    pallas_call x1, Pallas kernels: 96.7 us -> 94.1 us  [local(): pl.pallas_call(kernel, out_shape=jax.ShapeDtypeStruct((ROWS, CH), BF16),...]
where the time goes in v4:
time: 96 us; the launch traced here: 95.9 us
  Pallas kernels  94.1 us (98%)
  local copies, waits for them, and re-layouts  1.73 us (2%)
    pallas_call x1, Pallas kernels, local(): pl.pallas_call(kernel, out_shape=jax.ShapeDtypeStruct((ROWS, CH), BF16),...  94.1 us

profile of v4, /device:TPU:5, one launch (start us, length us, event | category | flops | bytes accessed | tf_op | source)
XLA Modules:
  0.0 95.9 jit_solution(4636898629557580299)
XLA Ops:
  0.0 0.0 copy-start
  0.0 0.0 copy-start.1
  0.0 0.0 copy-start.2
  0.0 0.0 copy-start.3
  0.0 0.0 copy-start.4
  0.0 1.0 %copy.9 = bf16[3,8,8,512]{3,2,0,1:T(8,128)(2,1)S(1)} copy(bf16[3,8,8,512]{3,2,1,0:T(8,128)(2,1)} %bitcast.5) | data formatting | bytes 393216 | tf_op jit(solution)/shard_map/reshape | solution.py:496
  1.0 0.0 copy-done
  1.0 0.0 copy-done.1
  1.0 0.0 copy-done.2
  1.1 0.0 copy-done.3
  1.1 0.0 copy-done.4
  1.1 94.1 %shard_map.64 = bf16[256,512]{1,0:T(8,128)(2,1)S(1)} custom-call(bf16[256,512]{1,0:T(8,128)(2,1)S(1)} %copy-done, bf16[64,1536]{1,0:T(8,128)(2,1)S(1)} %bitcast.3, f32[3,3,512]{2,1,0:T(4,128)S(1)} %copy-done.3, f32[16,512]{1,0:T(8,128)S(1)} %copy-done.1, f32[16,512]{1,0:T(8,128)S(1)} %copy-done.2, f32[1,512]{1,0:T(1,128)S(1)} %bitcast.4), custom_call_target="tpu_custom_call" | custom-call | tf_op jit(solution)/shard_map/pallas_call | solution.py:473
  95.2 0.7 copy.11
Async XLA Ops:
  0.0 1.0 %copy-start = (bf16[256,512]{1,0:T(8,128)(2,1)S(1)}, bf16[256,512]{1,0:T(8,128)(2,1)}, u32[]{:S(2)}) copy-start(bf16[256,512]{1,0:T(8,128)(2,1)} %tok.1) | copy-start | bytes 786436
  0.0 1.0 %copy-start.1 = (f32[16,512]{1,0:T(8,128)S(1)}, f32[16,512]{1,0:T(8,128)}, u32[]{:S(2)}) copy-start(f32[16,512]{1,0:T(8,128)} %res.1) | copy-start | bytes 98308
  0.0 1.0 %copy-start.2 = (f32[16,512]{1,0:T(8,128)S(1)}, f32[16,512]{1,0:T(8,128)}, u32[]{:S(2)}) copy-start(f32[16,512]{1,0:T(8,128)} %poles.1) | copy-start | bytes 98308
  0.0 1.0 %copy-start.3 = (f32[3,3,512]{2,1,0:T(4,128)S(1)}, f32[3,3,512]{2,1,0:T(4,128)}, u32[]{:S(2)}) copy-start(f32[3,3,512]{2,1,0:T(4,128)} %taps.1) | copy-start | bytes 55300
  0.0 1.0 %copy-start.4 = (f32[512]{0:T(512)S(1)}, f32[512]{0:T(512)}, u32[]{:S(2)}) copy-start(f32[512]{0:T(512)} %param.11) | copy-start | bytes 6148

commit v5 on v4

--- a/solution.py
+++ b/solution.py
@@ -15,7 +15,7 @@
 SUBS = 8
 STEPS = ROWS // SUBS
 TOP = 16
-SENDS, RECVS = 68, 81
+SENDS, RECVS = 44, 81
 
 
 def rounded(value):
@@ -94,10 +94,12 @@
             done.append(copy)
 
     def drain_groups():
+        for copy, cond in chained.values():
+            pl.when(cond)(lambda copy=copy: copy.wait_send())
         for group, blocks in (("leg", 2), ("near", 4), ("far", 2), ("turned", 16), ("passed", 8), ("sib", 32)):
             of_group(blocks, out_group=group).wait_send()
 
-    chain = {}
+    chain, chained = {}, {}
 
     def pass_along(j, key, ref):
         low, high = lax.rem(c - j + 9, 8), lax.rem(c + j - 1, 8)
@@ -105,7 +107,12 @@
             (0, low, up, (c < 7) & (c >= j - 1)),
             (1, high, dn, (c > 0) & (c + j <= 8)),
         ):
-            chain[j, key, way] = start(ref(block), ref(block), (s, to), cond)
+            if (j - 3, key, way) in chain:
+                before_cond = (c < 7) & (c >= j - 4) if way == 0 else (c > 0) & (c + j <= 11)
+                old = chain[j - 3, key, way]
+                pl.when(before_cond)(lambda: old.wait_send())
+            chain[j, key, way] = start(ref(block), ref(block), (s, to), cond, ("chain", j % 3, key, way))
+            chained[j % 3, key, way] = chain[j, key, way], cond
 
     def arrive(j, key):
         pl.when(c >= j)(lambda: chain[j, key, 0].wait_recv())
@@ -312,11 +319,11 @@
     tok_step(5, 1)
     last_step(5)
     dots(dot_z, zh, 4, 6)
-    theirs.wait_sibling()
-    dots(dot_z, 1 - zh, 0, 6)
     tok_step(6, 0)
     tok_step(6, 1)
     last_step(6)
+    theirs.wait_sibling()
+    dots(dot_z, 1 - zh, 0, 6)
     dots(dot_z, zh, 6, 7)
     dots(dot_z, 1 - zh, 6, 7)
     tok_step(7, 0)

time: 96 us -> 95.5 us (level)
  no operation moved by 1% of the time
where the time goes in v5:
time: 95.5 us; the launch traced here: 95.4 us
  Pallas kernels  93.6 us (98%)
  local copies, waits for them, and re-layouts  1.73 us (2%)
    pallas_call x1, Pallas kernels, local(): pl.pallas_call(kernel, out_shape=jax.ShapeDtypeStruct((ROWS, CH), BF16),...  93.6 us

profile of v5, /device:TPU:5, one launch (start us, length us, event | category | flops | bytes accessed | tf_op | source)
XLA Modules:
  0.0 95.4 jit_solution(16320400383004233970)
XLA Ops:
  0.0 0.0 copy-start
  0.0 0.0 copy-start.1
  0.0 0.0 copy-start.2
  0.0 0.0 copy-start.3
  0.0 0.0 copy-start.4
  0.0 1.0 %copy.9 = bf16[3,8,8,512]{3,2,0,1:T(8,128)(2,1)S(1)} copy(bf16[3,8,8,512]{3,2,1,0:T(8,128)(2,1)} %bitcast.5) | data formatting | bytes 393216 | tf_op jit(solution)/shard_map/reshape | solution.py:503
  1.0 0.0 copy-done
  1.0 0.0 copy-done.1
  1.0 0.0 copy-done.2
  1.1 0.0 copy-done.3
  1.1 0.0 copy-done.4
  1.1 93.6 %shard_map.64 = bf16[256,512]{1,0:T(8,128)(2,1)S(1)} custom-call(bf16[256,512]{1,0:T(8,128)(2,1)S(1)} %copy-done, bf16[64,1536]{1,0:T(8,128)(2,1)S(1)} %bitcast.3, f32[3,3,512]{2,1,0:T(4,128)S(1)} %copy-done.3, f32[16,512]{1,0:T(8,128)S(1)} %copy-done.1, f32[16,512]{1,0:T(8,128)S(1)} %copy-done.2, f32[1,512]{1,0:T(1,128)S(1)} %bitcast.4), custom_call_target="tpu_custom_call" | custom-call | tf_op jit(solution)/shard_map/pallas_call | solution.py:480
  94.7 0.7 copy.11
Async XLA Ops:
  0.0 1.0 %copy-start = (bf16[256,512]{1,0:T(8,128)(2,1)S(1)}, bf16[256,512]{1,0:T(8,128)(2,1)}, u32[]{:S(2)}) copy-start(bf16[256,512]{1,0:T(8,128)(2,1)} %tok.1) | copy-start | bytes 786436
  0.0 1.0 %copy-start.1 = (f32[16,512]{1,0:T(8,128)S(1)}, f32[16,512]{1,0:T(8,128)}, u32[]{:S(2)}) copy-start(f32[16,512]{1,0:T(8,128)} %res.1) | copy-start | bytes 98308
  0.0 1.0 %copy-start.2 = (f32[16,512]{1,0:T(8,128)S(1)}, f32[16,512]{1,0:T(8,128)}, u32[]{:S(2)}) copy-start(f32[16,512]{1,0:T(8,128)} %poles.1) | copy-start | bytes 98308
  0.0 1.0 %copy-start.3 = (f32[3,3,512]{2,1,0:T(4,128)S(1)}, f32[3,3,512]{2,1,0:T(4,128)}, u32[]{:S(2)}) copy-start(f32[3,3,512]{2,1,0:T(4,128)} %taps.1) | copy-start | bytes 55300
  0.0 1.0 %copy-start.4 = (f32[512]{0:T(512)S(1)}, f32[512]{0:T(512)}, u32[]{:S(2)}) copy-start(f32[512]{0:T(512)} %param.11) | copy-start | bytes 6148

commit v6 on v5

--- a/solution.py
+++ b/solution.py
@@ -365,7 +365,7 @@
             return k0, k1, v0, v1, tuple(a[n] * st[n] + g for n in range(MODES))
 
         zero = tuple(jnp.zeros((SUBS, 128), F32) for _ in range(MODES))
-        held = lax.fori_loop(0, STEPS, body, (lk(TOP - 1), lk(TOP - 2), lv(TOP - 1), lv(TOP - 2), zero), unroll=4)
+        held = lax.fori_loop(0, STEPS, body, (lk(TOP - 1), lk(TOP - 2), lv(TOP - 1), lv(TOP - 2), zero), unroll=8)
         for n in range(MODES):
             ends[n, :, lanes(lg)] = held[4][n]
             state[n : n + 1, lanes(lg)] = jnp.sum(tail_w[n, :, lanes(lg)] * held[4][n], axis=0, keepdims=True)
@@ -452,7 +452,7 @@
             obuf[lg, pl.ds(i, SUBS, stride=STEPS), :] = qbuf[i, :, lanes(lg)] * value
             return ws
 
-        lax.fori_loop(0, STEPS, body, ws, unroll=4)
+        lax.fori_loop(0, STEPS, body, ws, unroll=8)
         out[:, lanes(lg)] = obuf[lg].astype(BF16)
 
     for lg in own_groups:

time: 95.5 us -> 95.4 us (level)
  no operation moved by 1% of the time
where the time goes in v6:
time: 95.4 us; the launch traced here: 95.3 us
  Pallas kernels  93.5 us (98%)
  local copies, waits for them, and re-layouts  1.73 us (2%)
    pallas_call x1, Pallas kernels, local(): pl.pallas_call(kernel, out_shape=jax.ShapeDtypeStruct((ROWS, CH), BF16),...  93.5 us

profile of v6, /device:TPU:5, one launch (start us, length us, event | category | flops | bytes accessed | tf_op | source)
XLA Modules:
  0.0 95.3 jit_solution(2927779099039363475)
XLA Ops:
  0.0 0.0 copy-start
  0.0 0.0 copy-start.1
  0.0 0.0 copy-start.2
  0.0 0.0 copy-start.3
  0.0 0.0 copy-start.4
  0.0 1.0 %copy.9 = bf16[3,8,8,512]{3,2,0,1:T(8,128)(2,1)S(1)} copy(bf16[3,8,8,512]{3,2,1,0:T(8,128)(2,1)} %bitcast.5) | data formatting | bytes 393216 | tf_op jit(solution)/shard_map/reshape | solution.py:503
  1.0 0.0 copy-done
  1.0 0.0 copy-done.1
  1.0 0.0 copy-done.2
  1.1 0.0 copy-done.3
  1.1 0.0 copy-done.4
  1.1 93.5 %shard_map.64 = bf16[256,512]{1,0:T(8,128)(2,1)S(1)} custom-call(bf16[256,512]{1,0:T(8,128)(2,1)S(1)} %copy-done, bf16[64,1536]{1,0:T(8,128)(2,1)S(1)} %bitcast.3, f32[3,3,512]{2,1,0:T(4,128)S(1)} %copy-done.3, f32[16,512]{1,0:T(8,128)S(1)} %copy-done.1, f32[16,512]{1,0:T(8,128)S(1)} %copy-done.2, f32[1,512]{1,0:T(1,128)S(1)} %bitcast.4), custom_call_target="tpu_custom_call" | custom-call | tf_op jit(solution)/shard_map/pallas_call | solution.py:480
  94.6 0.7 copy.11
Async XLA Ops:
  0.0 1.0 %copy-start = (bf16[256,512]{1,0:T(8,128)(2,1)S(1)}, bf16[256,512]{1,0:T(8,128)(2,1)}, u32[]{:S(2)}) copy-start(bf16[256,512]{1,0:T(8,128)(2,1)} %tok.1) | copy-start | bytes 786436
  0.0 1.0 %copy-start.1 = (f32[16,512]{1,0:T(8,128)S(1)}, f32[16,512]{1,0:T(8,128)}, u32[]{:S(2)}) copy-start(f32[16,512]{1,0:T(8,128)} %res.1) | copy-start | bytes 98308
  0.0 1.0 %copy-start.2 = (f32[16,512]{1,0:T(8,128)S(1)}, f32[16,512]{1,0:T(8,128)}, u32[]{:S(2)}) copy-start(f32[16,512]{1,0:T(8,128)} %poles.1) | copy-start | bytes 98308
  0.0 1.0 %copy-start.3 = (f32[3,3,512]{2,1,0:T(4,128)S(1)}, f32[3,3,512]{2,1,0:T(4,128)}, u32[]{:S(2)}) copy-start(f32[3,3,512]{2,1,0:T(4,128)} %taps.1) | copy-start | bytes 55300
  0.0 1.0 %copy-start.4 = (f32[512]{0:T(512)S(1)}, f32[512]{0:T(512)}, u32[]{:S(2)}) copy-start(f32[512]{0:T(512)} %param.11) | copy-start | bytes 6148
